TPU v7x, 256 devices: a whole 4x4x8 slice. The times are simulated.
256 devices in a mesh: section: 32 (over x_hi, z, core), tensor: 8 (over y, x_lo).
Axes of the slice: x: 4 (x_hi: 2, x_lo: 2; x = x_hi * 2 + x_lo), y: 4, z: 8, core: 2. Of those that a mesh axis runs over, the one named last changes fastest.
Arguments:
- x_in: bfloat16 [32, 256, 12288], P('section', None, 'tensor'), may hold values from -6 to 6
- grad_in: bfloat16 [32, 256, 12288], P('section', None, 'tensor'), may hold values from -8 to 8
- stash_near: bfloat16 [32, 256, 12288], P('section', None, 'tensor'), may hold values from -8 to 8
- parked_in: bfloat16 [32, 256, 12288], P('section', None, 'tensor'), may hold values from -6 to 6
- fresh: bfloat16 [256, 12288], P(None, 'tensor'), may hold values from -6 to 6
- loss_grad: bfloat16 [256, 12288], P(None, 'tensor'), may hold values from -6 to 6
- gain: float32 [32, 12288], P('section', 'tensor'), may hold values from 0.1 to 1.9
- qgain: float32 [32, 12288], P('section', 'tensor'), may hold values from 0.25 to 450, as said below
- lengths: int32 [65], replicated, may hold values from 64 to 256, as said below
Outputs:
- forward_out: bfloat16 [32, 256, 12288], P('section', None, 'tensor')
- backward_out: bfloat16 [32, 256, 12288], P('section', None, 'tensor')
- parked_out: bfloat16 [32, 256, 12288], P('section', None, 'tensor')
- gain_grad: float32 [32, 12288], P('section', 'tensor')
- qgain_grad: float32 [32, 12288], P('section', 'tensor')
Inputs may be any that keep to these rules, and one draw needn't show every extreme that they name: `lengths`: every micro-batch keeps at least a quarter of its tokens; in every draw some micro-batch is full. `qgain`: positive query gains.
All inputs are finite; a program needn't handle non-finite values.
Results may differ from a plain program's by a relative error of at most 0.013.
The roundings to bfloat16 on the way count: a program that leaves them out, or rounds other values in their place, can miss the bound.
Values may be sent and summed in bfloat16 or wider, within the bound.
No kernel may reach another device: no remote copies, remote signals or barrier semaphores. Data moves between devices by JAX's collectives and lax.ppermute only.
A program may use at most 64 MiB of HBM per device.

v0:
```python
import jax
import jax.numpy as jnp
from jax import lax
from jax.sharding import PartitionSpec as P

D = 12288
HD = 128


epsilon = 1e-05


def swapped(value, axis, distance):
    return lax.ppermute(value, axis, [(i, i ^ 1 << distance) for i in range(lax.axis_size(axis))])


def passed_along(value, axis, by):
    count = lax.axis_size(axis)
    pairs = [(i, i + by) for i in range(count) if 0 <= i + by < count]
    return lax.ppermute(value, axis, pairs)


def allowed_mask(rows_n, length):
    row_ids = lax.broadcasted_iota(jnp.int32, (rows_n, rows_n), 0)
    col_ids = lax.broadcasted_iota(jnp.int32, (rows_n, rows_n), 1)
    return (col_ids <= row_ids) & (col_ids < length)


def attention_weights(query, hidden, length):
    scores = jnp.einsum("ihd,jhd->hij", query, hidden, preferred_element_type=jnp.float32) * (
        1.0 / HD
    )
    allowed = allowed_mask(query.shape[0], length)
    return jax.nn.softmax(jnp.where(allowed[None], scores, -jnp.inf), axis=-1)


def forward_local(in_float, inv_rms, gain_row, qgain_row, length):
    rows_n = in_float.shape[0]
    normed = in_float * inv_rms * gain_row
    hidden = normed.astype(jnp.bfloat16).reshape(rows_n, -1, HD)
    query = (normed * qgain_row).astype(jnp.bfloat16).reshape(rows_n, -1, HD)
    attend = attention_weights(query, hidden, length).astype(jnp.bfloat16)
    mixed = jnp.einsum("hij,jhd->ihd", attend, hidden, preferred_element_type=jnp.float32)
    return (in_float + mixed.reshape(rows_n, -1)).astype(jnp.bfloat16)


def backward_local(stored_float, inv_rms, out_grad, gain_row, qgain_row, length):
    rows_n = stored_float.shape[0]
    unit_rows = stored_float * inv_rms
    normed = unit_rows * gain_row
    hidden = normed.astype(jnp.bfloat16).reshape(rows_n, -1, HD)
    query = (normed * qgain_row).astype(jnp.bfloat16).reshape(rows_n, -1, HD)
    attend = attention_weights(query, hidden, length)
    attend_b = attend.astype(jnp.bfloat16)
    grad_heads = out_grad.reshape(rows_n, -1, HD)
    d_value = jnp.einsum("hij,ihd->jhd", attend_b, grad_heads, preferred_element_type=jnp.float32)
    d_attend = jnp.einsum("ihd,jhd->hij", grad_heads, hidden, preferred_element_type=jnp.float32)
    d_score = attend * (d_attend - jnp.sum(d_attend * attend, axis=-1, keepdims=True)) * (1.0 / HD)
    d_score = d_score.astype(jnp.bfloat16)
    d_query = jnp.einsum(
        "hij,jhd->ihd", d_score, hidden, preferred_element_type=jnp.float32
    ).reshape(rows_n, -1)
    d_key = jnp.einsum("hij,ihd->jhd", d_score, query, preferred_element_type=jnp.float32)
    d_normed = d_query * qgain_row + (d_key + d_value).reshape(rows_n, -1)
    qgain_part = jnp.sum(d_query * normed, axis=0)
    gain_part = jnp.sum(d_normed * unit_rows, axis=0)
    d_unit = d_normed * gain_row
    project = lax.psum(jnp.sum(d_unit * unit_rows, axis=-1), "tensor")[:, None] / D
    d_input = out_grad.astype(jnp.float32) + inv_rms * (d_unit - unit_rows * project)
    return (d_input.astype(jnp.bfloat16), gain_part, qgain_part)


def run_slot(fwd_input, stored, out_grad, gain_row, qgain_row, len_fwd, len_bwd):
    in_float = fwd_input.astype(jnp.float32)
    stored_float = stored.astype(jnp.float32)
    sum_fwd, sum_stored = lax.psum(
        (jnp.sum(in_float * in_float, axis=-1), jnp.sum(stored_float * stored_float, axis=-1)),
        "tensor",
    )
    inv_fwd = lax.rsqrt(sum_fwd[:, None] / D + epsilon)
    inv_stored = lax.rsqrt(sum_stored[:, None] / D + epsilon)
    layer_out = forward_local(in_float, inv_fwd, gain_row, qgain_row, len_fwd)
    d_input, gain_part, qgain_part = backward_local(
        stored_float, inv_stored, out_grad, gain_row, qgain_row, len_bwd
    )
    return (layer_out, d_input, gain_part, qgain_part)


def per_device(x_in, grad_in, stash_near, parked_in, fresh, loss_grad, gain, qgain, lengths):
    section_count = lax.axis_size("section")
    section_index = lax.axis_index("section")
    bit_count = section_count.bit_length() - 1
    bit_order = list(range(bit_count))
    gain_row = gain[0]
    qgain_row = qgain[0]
    fetched = parked_in[0]
    for bit_index in bit_order:
        fetched = swapped(fetched, "section", bit_index)
    first_out, first_grad, gain_one, qgain_one = run_slot(
        x_in[0],
        stash_near[0],
        grad_in[0],
        gain_row,
        qgain_row,
        lengths[2 * section_count - 1 - section_index],
        lengths[section_index],
    )
    arrived = passed_along(first_out, "section", 1)
    returned = passed_along(first_grad, "section", -1)
    x_two = jnp.where(section_index == 0, fresh, arrived)
    d_two = jnp.where(section_index == section_count - 1, loss_grad, returned)
    parked = x_two
    for bit_index in bit_order:
        parked = swapped(parked, "section", bit_index)
    second_out, second_grad, gain_two, qgain_two = run_slot(
        x_two,
        fetched,
        d_two,
        gain_row,
        qgain_row,
        lengths[2 * section_count - section_index],
        lengths[section_index + 1],
    )
    return (
        second_out[None],
        second_grad[None],
        parked[None],
        (gain_one + gain_two)[None],
        (qgain_one + qgain_two)[None],
    )


def solution(mesh):
    in_specs = (
        P("section", None, "tensor"),
        P("section", None, "tensor"),
        P("section", None, "tensor"),
        P("section", None, "tensor"),
        P(None, "tensor"),
        P(None, "tensor"),
        P("section", "tensor"),
        P("section", "tensor"),
        P(),
    )
    out_specs = (
        P("section", None, "tensor"),
        P("section", None, "tensor"),
        P("section", None, "tensor"),
        P("section", "tensor"),
        P("section", "tensor"),
    )
    return jax.shard_map(
        per_device, mesh=mesh, in_specs=in_specs, out_specs=out_specs, check_vma=False
    )
```

profile of v0, /device:TPU:1, one launch (start us, length us, event | category | flops | bytes accessed | tf_op | source)
XLA Modules:
  0.0 317.8 jit_solution(8892851261910596672)
XLA Ops:
  0.7 1.5 copy.67
  2.2 3.3 %collective-permute-start.2 = (bf16[256,1536]{0,1:T(8,128)(2,1)S(1)}, bf16[256,1536]{0,1:T(8,128)(2,1)}, u32[]{:S(2)}, u32[]{:S(2)}) collective-permute-start(bf16[256,1536]{0,1:T(8,128)(2,1)S(1)} %bitcast.157), channel_id=1, source_target_pairs={{0,8},{8,0},{16,24},{24,16},{32,40},{40,32},{48,56},{56,48},{64,72... | collective-permute-start | bytes 2359304 | tf_op jit(solution)/shard_map/ppermute | solution.py:14
  5.5 0.3 copy.57
  5.8 0.6 fusion.119
  6.4 0.2 fusion.53
  6.6 14.5 %psum.44 = f32[256]{0:T(256)S(1)} all-reduce(f32[256]{0:T(256)S(1)} %fusion.53), channel_id=1, replica_groups=mesh['section'=32,'tensor'=8] {'tensor'}, use_global_device_ids=true, to_apply=%region_9.10 | all-reduce | flops 256 | bytes 2048 | tf_op jit(solution)/shard_map/psum | solution.py:76
  21.1 0.6 iota_compare_fusion.2
  21.8 0.7 iota_compare_fusion.1
  22.6 1.7 collective-permute-start.3
  24.3 0.6 iota_compare_fusion.4
  25.0 0.3 copy.56
  25.3 0.3 copy.48
  25.8 1.4 multiply_convert_fusion.3
  27.2 11.4 %collective-permute-done.3 = bf16[256,1536]{0,1:T(8,128)(2,1)} collective-permute-done((bf16[256,1536]{0,1:T(8,128)(2,1)}, bf16[256,1536]{0,1:T(8,128)(2,1)}, u32[]{:S(2)}, u32[]{:S(2)}) %collective-permute-start.3) | collective-permute-done | bytes 786464 | tf_op jit(solution)/shard_map/ppermute | solution.py:14
  38.6 3.0 collective-permute-start.4
  41.6 0.6 iota_compare_fusion.3
  42.2 2.3 fusion.126
  44.5 4.5 %fusion.120 = (f32[12,256]{1,0:T(8,128)S(1)}, f32[12,256,256]{1,2,0:T(8,128)}) fusion(pred[256,256]{0,1:T(8,128)(4,1)S(1)} %fusion.94, bf16[256,12,128]{0,2,1:T(8,128)(2,1)S(1)} %get-tuple-element.24, f32[256,12,128]{0,2,1:T(8,128)} %get-tuple-element.25, f32[256]{0:T(256)S(1)} %add_rsqrt_fusion.1, f32[12,128]{1,0:T(8,128)S(1)} %bitcast.165, ...), kind=kOutput, calls=%fused_computation.157 | convolution fusion | flops 206045440 | bytes 5596160 | tf_op jit(solution)/shard_map/sub | solution.py:34
  49.1 25.3 %collective-permute-done.4 = bf16[256,1536]{0,1:T(8,128)(2,1)} collective-permute-done((bf16[256,1536]{0,1:T(8,128)(2,1)}, bf16[256,1536]{0,1:T(8,128)(2,1)}, u32[]{:S(2)}, u32[]{:S(2)}) %collective-permute-start.4) | collective-permute-done | bytes 786464 | tf_op jit(solution)/shard_map/ppermute | solution.py:14
  74.4 6.9 %collective-permute-start.5 = (bf16[256,1536]{0,1:T(8,128)(2,1)}, bf16[256,1536]{0,1:T(8,128)(2,1)}, u32[]{:S(2)}, u32[]{:S(2)}) collective-permute-start(bf16[256,1536]{0,1:T(8,128)(2,1)} %collective-permute-done.4), channel_id=1, source_target_pairs={{0,64},{8,72},{16,80},{24,88},{32,96},{40,104},{48,112},{56,120},{... | collective-permute-start | bytes 2359304 | tf_op jit(solution)/shard_map/ppermute | solution.py:14
  81.4 6.9 %fusion.84 = f32[12,128,256]{2,1,0:T(8,128)} fusion(bf16[256,12,128]{0,2,1:T(8,128)(2,1)S(1)} %get-tuple-element.24, f32[12,256,256]{2,1,0:T(8,128)} %fusion.126, f32[12,256,256]{1,2,0:T(8,128)} %get-tuple-element.37, f32[12,256]{1,0:T(8,128)S(1)} %get-tuple-element.36), kind=kOutput, calls=%fused_computation.110 | convolution fusion | flops 206834944 | bytes 8663040 | tf_op jit(solution)/shard_map/hij,jhd->ihd/dot_general | solution.py:60
  88.3 7.5 %fusion.83 = f32[12,128,256]{2,1,0:T(8,128)} fusion(f32[12,256,256]{2,1,0:T(8,128)} %fusion.126, f32[12,256,256]{1,2,0:T(8,128)} %get-tuple-element.37, f32[12,256]{1,0:T(8,128)S(1)} %get-tuple-element.36, f32[256,12,128]{0,2,1:T(8,128)} %get-tuple-element.25, f32[256]{0:T(256)S(1)} %add_rsqrt_fusion.1, f32[12,128]{1,0:T(8,128)S(1)} %bitcast.166, ...), kind=kOutput, calls=%fused_computation.109 | convolution fusion | flops 208407808 | bytes 9462784 | tf_op jit(solution)/shard_map/hij,ihd->jhd/dot_general | solution.py:63
  95.8 18.9 %collective-permute-done.5 = bf16[256,1536]{0,1:T(8,128)(2,1)} collective-permute-done((bf16[256,1536]{0,1:T(8,128)(2,1)}, bf16[256,1536]{0,1:T(8,128)(2,1)}, u32[]{:S(2)}, u32[]{:S(2)}) %collective-permute-start.5) | collective-permute-done | bytes 786464 | tf_op jit(solution)/shard_map/ppermute | solution.py:14
  114.7 2.5 collective-permute-start.6
  117.2 0.2 fusion.55
  117.4 2.3 copy.66
  119.7 2.3 copy.52
  122.0 5.6 %multiply_reduce_fusion.1 = (f32[12,128]{1,0:T(8,128)S(1)}, f32[256]{0:T(256)S(1)}, f32[12,128]{1,0:T(8,128)S(1)}, f32[256,12,128]{0,2,1:T(8,128)}) fusion(f32[256,12,128]{0,2,1:T(8,128)} %get-tuple-element.25, f32[256]{0:T(256)S(1)} %add_rsqrt_fusion.1, f32[12,128]{1,0:T(8,128)S(1)} %bitcast.167, f32[12,128,256]{2,1,0:T(8,128)} %fusion.84, ...), kind=kOutput, calls=%fused_computation.79 | convolution fusion | flops 207614720 | bytes 10262528 | tf_op jit(solution)/shard_map/hij,ihd->jhd/dot_general | solution.py:56
  127.6 5.4 %collective-permute-done.6 = bf16[256,1536]{0,1:T(8,128)(2,1)S(1)} collective-permute-done((bf16[256,1536]{0,1:T(8,128)(2,1)}, bf16[256,1536]{0,1:T(8,128)(2,1)S(1)}, u32[]{:S(2)}, u32[]{:S(2)}) %collective-permute-start.6) | collective-permute-done | bytes 786464 | tf_op jit(solution)/shard_map/ppermute | solution.py:14
  132.9 0.2 fusion.37
  133.2 13.7 %all-reduce.1 = (f32[256]{0:T(256)S(1)}, f32[256]{0:T(256)S(1)}, f32[256]{0:T(256)S(1)}) all-reduce(f32[256]{0:T(256)S(1)} %fusion.55, f32[256]{0:T(256)S(1)} %get-tuple-element.11, f32[256]{0:T(256)S(1)} %fusion.37), channel_id=1, replica_groups=mesh['section'=32,'tensor'=8] {'tensor'}, use_global_device_ids=true, to_apply=%region_1.0 | all-reduce | flops 768 | bytes 6144 | tf_op jit(solution)/shard_map/psum | solution.py:76
  146.9 3.6 %fusion.29 = (bf16[256,1536]{0,1:T(8,128)(2,1)}, bf16[256,1536]{0,1:T(8,128)(2,1)}, bf16[256,1536]{0,1:T(8,128)(2,1)}) fusion(bf16[256,1536]{0,1:T(8,128)(2,1)S(1)} %collective-permute-done.6, f32[256]{0:T(256)S(1)} %add_rsqrt_fusion, f32[1536]{0:T(1024)S(1)} %reduce.4, f32[1536]{0:T(1024)S(1)} %reduce.3, f32[256]{0:T(256)S(1)} %get-tuple-element.46, ...), kind=kLoop, calls=%fused_computation.42 | loop fusion | flops 6684672 | bytes 7879680 | tf_op jit(solution)/shard_map/convert_element_type | solution.py:52
  150.4 8.9 %collective-permute-start.1 = (bf16[256,1536]{0,1:T(8,128)(2,1)}, bf16[256,1536]{0,1:T(8,128)(2,1)}, u32[]{:S(2)}, u32[]{:S(2)}) collective-permute-start(bf16[256,1536]{0,1:T(8,128)(2,1)} %get-tuple-element.30), channel_id=1, source_target_pairs={{8,0},{16,8},{24,16},{32,24},{40,32},{48,40},{56,48},{64,56},{72,6... | collective-permute-start | bytes 2359304 | tf_op jit(solution)/shard_map/ppermute | solution.py:20
  159.3 1.2 fusion.85
  160.5 0.9 fusion.121
  161.5 0.5 fusion.70
  162.0 1.1 fusion.50
  163.2 1.9 collective-permute-start
  165.1 4.0 %fusion.122 = (f32[12,256]{1,0:T(8,128)S(1)}, f32[12,256,256]{1,2,0:T(8,128)}) fusion(pred[256,256]{0,1:T(8,128)(4,1)S(1)} %fusion.93, bf16[256,12,128]{0,2,1:T(8,128)(2,1)} %bitcast.152, bf16[256,12,128]{0,2,1:T(8,128)(2,1)S(1)} %bitcast.148), kind=kOutput, calls=%fused_computation.159 | convolution fusion | flops 204472576 | bytes 4796416 | tf_op jit(solution)/shard_map/sub | solution.py:34
  169.1 1.2 broadcast_select_fusion
  170.4 2.3 fusion.127
  172.7 1.6 collective-permute-done
  174.3 1.5 fusion.38
  175.9 6.8 %fusion.20 = f32[12,128,256]{2,1,0:T(8,128)} fusion(bf16[256,12,128]{0,2,1:T(8,128)(2,1)S(1)} %bitcast.150, f32[12,256,256]{1,2,0:T(8,128)} %fusion.127, f32[12,256,256]{1,2,0:T(8,128)} %get-tuple-element.42, f32[12,256]{1,0:T(8,128)S(1)} %get-tuple-element.41), kind=kOutput, calls=%fused_computation.32 | convolution fusion | flops 206834944 | bytes 8663040 | tf_op jit(solution)/shard_map/hij,jhd->ihd/dot_general | solution.py:60
  182.7 3.9 %fusion.56 = f32[12,128,256]{2,1,0:T(8,128)} fusion(bf16[256,12,128]{0,2,1:T(8,128)(2,1)S(1)} %bitcast.147, f32[12,256,256]{1,2,0:T(8,128)} %get-tuple-element.42, f32[12,256]{1,0:T(8,128)S(1)} %get-tuple-element.41), kind=kOutput, calls=%fused_computation.80 | convolution fusion | flops 202899456 | bytes 5517312 | tf_op jit(solution)/shard_map/hij,ihd->jhd/dot_general | solution.py:56
  186.6 7.4 %fusion.78 = f32[12,128,256]{2,1,0:T(8,128)} fusion(f32[12,128,256]{2,1,0:T(8,128)} %fusion.56, bf16[256,12,128]{0,2,1:T(8,128)(2,1)S(1)} %bitcast.153, f32[12,256,256]{1,2,0:T(8,128)} %fusion.127, f32[12,256,256]{1,2,0:T(8,128)} %get-tuple-element.42, f32[12,256]{1,0:T(8,128)S(1)} %get-tuple-element.41), kind=kOutput, calls=%fused_computation.106 | convolution fusion | flops 207228160 | bytes 10235904 | tf_op jit(solution)/shard_map/hij,ihd->jhd/dot_general | solution.py:63
  194.0 2.6 collective-permute-start.8
  196.6 3.5 %fusion.36 = (f32[1536]{0:T(1024)S(1)}, f32[256]{0:T(256)S(1)}, f32[1536]{0:T(1024)S(1)}, f32[256,1536]{0,1:T(8,128)}) fusion(bf16[256,1536]{0,1:T(8,128)(2,1)S(1)} %collective-permute-done.6, f32[256]{0:T(256)S(1)} %add_rsqrt_fusion, f32[1536]{0:T(1024)S(1)} %reduce.3, f32[12,128,256]{2,1,0:T(8,128)} %fusion.20, f32[12,128,256]{2,1,0:T(8,128)} %fusion.78, ...), kind=kLoop, calls=%fused_computation.49 | loop fusion | flops 4715264 | bytes 5531648 | tf_op jit(solution)/shard_map/reduce_sum | solution.py:66
  200.1 13.4 %all-reduce = (f32[256]{0:T(256)S(1)}, f32[256]{0:T(256)S(1)}) all-reduce(f32[256]{0:T(256)S(1)} %get-tuple-element.22, f32[256]{0:T(256)S(1)} %get-tuple-element.14), channel_id=1, replica_groups=mesh['section'=32,'tensor'=8] {'tensor'}, use_global_device_ids=true, to_apply=%region_5.6 | all-reduce | flops 512 | bytes 4096 | tf_op jit(solution)/shard_map/psum | solution.py:76
  213.5 1.3 collective-permute-done.8
  214.8 5.1 %collective-permute-start.9 = (bf16[256,1536]{0,1:T(8,128)(2,1)}, bf16[256,1536]{0,1:T(8,128)(2,1)}, u32[]{:S(2)}, u32[]{:S(2)}) collective-permute-start(bf16[256,1536]{0,1:T(8,128)(2,1)} %collective-permute-done.8), channel_id=1, source_target_pairs={{0,32},{8,40},{16,48},{24,56},{32,0},{40,8},{48,16},{56,24},{64,96... | collective-permute-start | bytes 2359304 | tf_op jit(solution)/shard_map/ppermute | solution.py:14
  219.9 3.0 fusion.42
  223.0 4.3 %fusion.123 = (f32[12,256]{1,0:T(8,128)S(1)}, f32[12,256,256]{1,2,0:T(8,128)}) fusion(pred[256,256]{0,1:T(8,128)(4,1)S(1)} %fusion.95, bf16[256,12,128]{0,2,1:T(8,128)(2,1)} %bitcast.156, bf16[256,12,128]{0,2,1:T(8,128)(2,1)} %bitcast.154), kind=kOutput, calls=%fused_computation.160 | convolution fusion | flops 204472576 | bytes 4796416 | tf_op jit(solution)/shard_map/sub | solution.py:34
  227.3 26.8 %collective-permute-done.9 = bf16[256,1536]{0,1:T(8,128)(2,1)} collective-permute-done((bf16[256,1536]{0,1:T(8,128)(2,1)}, bf16[256,1536]{0,1:T(8,128)(2,1)}, u32[]{:S(2)}, u32[]{:S(2)}) %collective-permute-start.9) | collective-permute-done | bytes 786464 | tf_op jit(solution)/shard_map/ppermute | solution.py:14
  254.1 5.3 %collective-permute-start.10 = (bf16[256,1536]{0,1:T(8,128)(2,1)}, bf16[256,1536]{0,1:T(8,128)(2,1)S(1)}, u32[]{:S(2)}, u32[]{:S(2)}) collective-permute-start(bf16[256,1536]{0,1:T(8,128)(2,1)} %collective-permute-done.9), channel_id=1, source_target_pairs={{0,64},{8,72},{16,80},{24,88},{32,96},{40,104},{48,112},{56,120},{... | collective-permute-start | bytes 2359304 | tf_op jit(solution)/shard_map/ppermute | solution.py:14
  259.4 2.3 fusion.71
  261.9 1.2 copy.75
  263.1 1.2 copy.76
  264.2 28.6 %collective-permute-done.10 = bf16[256,1536]{0,1:T(8,128)(2,1)S(1)} collective-permute-done((bf16[256,1536]{0,1:T(8,128)(2,1)}, bf16[256,1536]{0,1:T(8,128)(2,1)S(1)}, u32[]{:S(2)}, u32[]{:S(2)}) %collective-permute-start.10) | collective-permute-done | bytes 786464 | tf_op jit(solution)/shard_map/ppermute | solution.py:14
  292.8 6.4 %collective-permute-start.11 = (bf16[256,1536]{0,1:T(8,128)(2,1)S(1)}, bf16[256,1536]{0,1:T(8,128)(2,1)S(1)}, u32[]{:S(2)}, u32[]{:S(2)}) collective-permute-start(bf16[256,1536]{0,1:T(8,128)(2,1)S(1)} %collective-permute-done.10), channel_id=1, source_target_pairs={{0,128},{8,136},{16,144},{24,152},{32,160},{40,168},{48,176},{56,1... | collective-permute-start | bytes 2359304 | tf_op jit(solution)/shard_map/ppermute | solution.py:14
  299.2 0.6 bitcast_add_fusion.3
  299.8 0.6 bitcast_add_fusion.4
  300.4 16.3 %collective-permute-done.11 = bf16[256,1536]{0,1:T(8,128)(2,1)S(1)} collective-permute-done((bf16[256,1536]{0,1:T(8,128)(2,1)S(1)}, bf16[256,1536]{0,1:T(8,128)(2,1)S(1)}, u32[]{:S(2)}, u32[]{:S(2)}) %collective-permute-start.11) | collective-permute-done | bytes 786464 | tf_op jit(solution)/shard_map/ppermute | solution.py:14
  316.7 1.2 copy.77
  (38 shorter events, 0.9 us)
Async XLA Ops:
  0.6 4.9 %copy-start.5 = (bf16[1,256,1536]{2,1,0:T(8,128)(2,1)S(1)}, bf16[1,256,1536]{2,1,0:T(8,128)(2,1)}, u32[]{:S(2)}) copy-start(bf16[1,256,1536]{2,1,0:T(8,128)(2,1)} %param.11) | copy-start | bytes 2359300
  0.6 5.1 %copy-start.8 = (s32[65]{0:T(128)S(1)}, s32[65]{0:T(128)}, u32[]{:S(2)}) copy-start(s32[65]{0:T(128)} %param.17) | copy-start | bytes 784
  2.1 22.8 %copy-start.9 = (f32[1,1536]{1,0:T(1,128)S(1)}, f32[1,1536]{1,0:T(1,128)}, u32[]{:S(2)}) copy-start(f32[1,1536]{1,0:T(1,128)} %param.15) | copy-start | bytes 18436
  2.1 22.8 %copy-start.10 = (f32[1,1536]{1,0:T(1,128)S(1)}, f32[1,1536]{1,0:T(1,128)}, u32[]{:S(2)}) copy-start(f32[1,1536]{1,0:T(1,128)} %param.16) | copy-start | bytes 18436
  2.2 22.9 %copy-start.6 = (bf16[1,256,1536]{2,1,0:T(8,128)(2,1)S(1)}, bf16[1,256,1536]{2,1,0:T(8,128)(2,1)}, u32[]{:S(2)}) copy-start(bf16[1,256,1536]{2,1,0:T(8,128)(2,1)} %param.10) | copy-start | bytes 2359300
  2.2 20.4 %collective-permute-start.2 = (bf16[256,1536]{0,1:T(8,128)(2,1)S(1)}, bf16[256,1536]{0,1:T(8,128)(2,1)}, u32[]{:S(2)}, u32[]{:S(2)}) collective-permute-start(bf16[256,1536]{0,1:T(8,128)(2,1)S(1)} %bitcast.157), channel_id=1, source_target_pairs={{0,8},{8,0},{16,24},{24,16},{32,40},{40,32},{48,56},{56,48},{64,72... | collective-permute-start | bytes 2359304 | tf_op jit(solution)/shard_map/ppermute | solution.py:14
  5.8 19.5 %copy-start.7 = (bf16[1,256,1536]{2,1,0:T(8,128)(2,1)S(1)}, bf16[1,256,1536]{2,1,0:T(8,128)(2,1)}, u32[]{:S(2)}) copy-start(bf16[1,256,1536]{2,1,0:T(8,128)(2,1)} %param.9) | copy-start | bytes 2359300
  22.6 16.0 %collective-permute-start.3 = (bf16[256,1536]{0,1:T(8,128)(2,1)}, bf16[256,1536]{0,1:T(8,128)(2,1)}, u32[]{:S(2)}, u32[]{:S(2)}) collective-permute-start(bf16[256,1536]{0,1:T(8,128)(2,1)} %collective-permute-done.2), channel_id=1, source_target_pairs={{0,16},{8,24},{16,0},{24,8},{32,48},{40,56},{48,32},{56,40},{64,80... | collective-permute-start | bytes 2359304 | tf_op jit(solution)/shard_map/ppermute | solution.py:14
  38.6 35.8 %collective-permute-start.4 = (bf16[256,1536]{0,1:T(8,128)(2,1)}, bf16[256,1536]{0,1:T(8,128)(2,1)}, u32[]{:S(2)}, u32[]{:S(2)}) collective-permute-start(bf16[256,1536]{0,1:T(8,128)(2,1)} %collective-permute-done.3), channel_id=1, source_target_pairs={{0,32},{8,40},{16,48},{24,56},{32,0},{40,8},{48,16},{56,24},{64,96... | collective-permute-start | bytes 2359304 | tf_op jit(solution)/shard_map/ppermute | solution.py:14
  74.4 40.4 %collective-permute-start.5 = (bf16[256,1536]{0,1:T(8,128)(2,1)}, bf16[256,1536]{0,1:T(8,128)(2,1)}, u32[]{:S(2)}, u32[]{:S(2)}) collective-permute-start(bf16[256,1536]{0,1:T(8,128)(2,1)} %collective-permute-done.4), channel_id=1, source_target_pairs={{0,64},{8,72},{16,80},{24,88},{32,96},{40,104},{48,112},{56,120},{... | collective-permute-start | bytes 2359304 | tf_op jit(solution)/shard_map/ppermute | solution.py:14
  114.7 18.2 %collective-permute-start.6 = (bf16[256,1536]{0,1:T(8,128)(2,1)}, bf16[256,1536]{0,1:T(8,128)(2,1)S(1)}, u32[]{:S(2)}, u32[]{:S(2)}) collective-permute-start(bf16[256,1536]{0,1:T(8,128)(2,1)} %collective-permute-done.5), channel_id=1, source_target_pairs={{0,128},{8,136},{16,144},{24,152},{32,160},{40,168},{48,176},{56,1... | collective-permute-start | bytes 2359304 | tf_op jit(solution)/shard_map/ppermute | solution.py:14
  150.4 18.7 %collective-permute-start.1 = (bf16[256,1536]{0,1:T(8,128)(2,1)}, bf16[256,1536]{0,1:T(8,128)(2,1)}, u32[]{:S(2)}, u32[]{:S(2)}) collective-permute-start(bf16[256,1536]{0,1:T(8,128)(2,1)} %get-tuple-element.30), channel_id=1, source_target_pairs={{8,0},{16,8},{24,16},{32,24},{40,32},{48,40},{56,48},{64,56},{72,6... | collective-permute-start | bytes 2359304 | tf_op jit(solution)/shard_map/ppermute | solution.py:20
  162.0 3.1 copy-start
  163.2 11.1 %collective-permute-start = (bf16[256,1536]{0,1:T(8,128)(2,1)}, bf16[256,1536]{0,1:T(8,128)(2,1)}, u32[]{:S(2)}, u32[]{:S(2)}) collective-permute-start(bf16[256,1536]{0,1:T(8,128)(2,1)} %fusion.50), channel_id=1, source_target_pairs={{0,8},{8,16},{16,24},{24,32},{32,40},{40,48},{48,56},{56,64},{64,7... | collective-permute-start | bytes 2359304 | tf_op jit(solution)/shard_map/ppermute | solution.py:20
  165.1 4.0 %copy-start.1 = (bf16[256,1536]{0,1:T(8,128)(2,1)S(1)}, bf16[256,1536]{0,1:T(8,128)(2,1)}, u32[]{:S(2)}) copy-start(bf16[256,1536]{0,1:T(8,128)(2,1)} %copy.66) | copy-start | bytes 2359300
  170.4 4.0 %copy-start.2 = (bf16[256,1536]{0,1:T(8,128)(2,1)S(1)}, bf16[256,1536]{0,1:T(8,128)(2,1)}, u32[]{:S(2)}) copy-start(bf16[256,1536]{0,1:T(8,128)(2,1)} %copy.52) | copy-start | bytes 2359300
  175.8 18.2 %collective-permute-start.7 = (bf16[256,1536]{0,1:T(8,128)(2,1)S(1)}, bf16[256,1536]{0,1:T(8,128)(2,1)}, u32[]{:S(2)}, u32[]{:S(2)}) collective-permute-start(bf16[256,1536]{0,1:T(8,128)(2,1)S(1)} %get-tuple-element.23), channel_id=1, source_target_pairs={{0,8},{8,0},{16,24},{24,16},{32,40},{40,32},{48,56},{56,48},{64,72... | collective-permute-start | bytes 2359304 | tf_op jit(solution)/shard_map/ppermute | solution.py:14
  182.7 3.9 %copy-start.3 = (bf16[256,1536]{0,1:T(8,128)(2,1)S(1)}, bf16[256,1536]{0,1:T(8,128)(2,1)}, u32[]{:S(2)}) copy-start(bf16[256,1536]{0,1:T(8,128)(2,1)} %get-tuple-element.28) | copy-start | bytes 2359300
  194.0 20.8 %collective-permute-start.8 = (bf16[256,1536]{0,1:T(8,128)(2,1)}, bf16[256,1536]{0,1:T(8,128)(2,1)}, u32[]{:S(2)}, u32[]{:S(2)}) collective-permute-start(bf16[256,1536]{0,1:T(8,128)(2,1)} %collective-permute-done.7), channel_id=1, source_target_pairs={{0,16},{8,24},{16,0},{24,8},{32,48},{40,56},{48,32},{56,40},{64,80... | collective-permute-start | bytes 2359304 | tf_op jit(solution)/shard_map/ppermute | solution.py:14
  214.8 39.3 %collective-permute-start.9 = (bf16[256,1536]{0,1:T(8,128)(2,1)}, bf16[256,1536]{0,1:T(8,128)(2,1)}, u32[]{:S(2)}, u32[]{:S(2)}) collective-permute-start(bf16[256,1536]{0,1:T(8,128)(2,1)} %collective-permute-done.8), channel_id=1, source_target_pairs={{0,32},{8,40},{16,48},{24,56},{32,0},{40,8},{48,16},{56,24},{64,96... | collective-permute-start | bytes 2359304 | tf_op jit(solution)/shard_map/ppermute | solution.py:14
  223.0 36.4 %copy-start.4 = (bf16[256,1536]{0,1:T(8,128)(2,1)S(1)}, bf16[256,1536]{0,1:T(8,128)(2,1)}, u32[]{:S(2)}) copy-start(bf16[256,1536]{0,1:T(8,128)(2,1)} %get-tuple-element.27) | copy-start | bytes 2359300
  254.1 38.8 %collective-permute-start.10 = (bf16[256,1536]{0,1:T(8,128)(2,1)}, bf16[256,1536]{0,1:T(8,128)(2,1)S(1)}, u32[]{:S(2)}, u32[]{:S(2)}) collective-permute-start(bf16[256,1536]{0,1:T(8,128)(2,1)} %collective-permute-done.9), channel_id=1, source_target_pairs={{0,64},{8,72},{16,80},{24,88},{32,96},{40,104},{48,112},{56,120},{... | collective-permute-start | bytes 2359304 | tf_op jit(solution)/shard_map/ppermute | solution.py:14
  292.8 23.9 %collective-permute-start.11 = (bf16[256,1536]{0,1:T(8,128)(2,1)S(1)}, bf16[256,1536]{0,1:T(8,128)(2,1)S(1)}, u32[]{:S(2)}, u32[]{:S(2)}) collective-permute-start(bf16[256,1536]{0,1:T(8,128)(2,1)S(1)} %collective-permute-done.10), channel_id=1, source_target_pairs={{0,128},{8,136},{16,144},{24,152},{32,160},{40,168},{48,176},{56,1... | collective-permute-start | bytes 2359304 | tf_op jit(solution)/shard_map/ppermute | solution.py:14
where the time goes:
time: 319 us; the launch traced here: 318 us
  waiting for transfers between devices  136 us (43%)
  matrix products  59.6 us (19%)
  starting transfers between devices  47.7 us (15%)
  blocking collectives  41.6 us (13%)
  other arithmetic  21.4 us (7%)
  local copies, waits for them, and re-layouts  11 us (3%)
    ppermute x10, waiting for transfers between devices, swapped(): lax.ppermute(value, axis, [(i, i ^ 1 << distance) for i in range(lax.axis...  134 us
    psum x3, blocking collectives, run_slot(): lax.psum((jnp.sum(in_float * in_float, axis=-1), jnp.sum(stored_float * s...  41.6 us
    ppermute x10, starting transfers between devices, swapped(): lax.ppermute(value, axis, [(i, i ^ 1 << distance) for i in range(lax.axis...  36.9 us
    dot_general x2, matrix products, backward_local(): jnp.einsum('hij,ihd->jhd', d_score, query, preferred_element_type=jnp.flo...  14.9 us
    dot_general x2, matrix products, backward_local(): jnp.einsum('hij,jhd->ihd', d_score, hidden, preferred_element_type=jnp.fl...  13.8 us
    sub x3, matrix products, attention_weights(): return jax.nn.softmax(jnp.where(allowed[None], scores, -jnp.inf), axis=-1)  12.8 us
    ppermute x2, starting transfers between devices, passed_along(): return lax.ppermute(value, axis, pairs)  10.8 us
    unnamed x31, local copies, waits for them, and re-layouts  10.4 us
  transfers between devices with their start and end apart: 12, of which 9 were waited for; matrix products, arithmetic and copies ran while one was open for 26% of the time, Pallas kernels for 0%

commit v1 on v0

v1 whole, which is shorter than its diff:
```python
import functools

import jax
import jax.numpy as jnp
from jax import lax
from jax.experimental import pallas as pl
from jax.experimental.pallas import tpu as pltpu
from jax.sharding import PartitionSpec as P

D = 12288
HD = 128
TOK = 256
HALF = 128
EPSILON = 1e-05
LOG2E = 1.4426950408889634
MASKED = -1e30
VMEM_LIMIT = 40 * 1024 * 1024
UNROLL = 6
COST = 1.0
MIRROR_ROWS = (256,)
AFTER = ((), (), ('m0', 'tm', 'x', ), (), (), (), ())
PARK_ROWS = (256,)
LAST = True

ROWS_ROWS = (((1,), (1,)), ((), ()))
COLS_ROWS = (((0,), (0,)), ((), ()))
PLAIN = (((1,), (0,)), ((), ()))


def matmul(left, right, dims):
    return lax.dot_general(left, right, dims, preferred_element_type=jnp.float32)


def token_row(per_lane):
    return jnp.sum(per_lane.T, axis=0, keepdims=True)


def token_columns(row):
    return jnp.broadcast_to(row, (HD, TOK)).T


def gathered_row(sums_ref, k):
    return jnp.sum(sums_ref[:, k, :], axis=0, keepdims=True)


def inverse_rms(sum_row):
    return lax.rsqrt(sum_row / D + EPSILON)


def head_columns(h):
    return pl.ds(pl.multiple_of(h * HD, HD), HD)


def over_heads(count, body, init=None):
    def step(i, carry):
        for u in range(UNROLL):
            carry = body(i * UNROLL + u, carry)
        return carry

    return lax.fori_loop(0, count // UNROLL, step, init)


def fill_bias(bias, length):
    key = lax.broadcasted_iota(jnp.int32, (TOK, TOK), 0)
    query = lax.broadcasted_iota(jnp.int32, (TOK, TOK), 1)
    bias[...] = jnp.where((key <= query) & (key < length), 0.0, MASKED)


def attention(hidden, query, bias):
    low = matmul(hidden[:HALF], query, ROWS_ROWS) + bias[:HALF, :]
    high = matmul(hidden[HALF:], query[HALF:], ROWS_ROWS) + bias[HALF:, HALF:]
    top_low = jnp.max(low, axis=0, keepdims=True)
    top_high = jnp.maximum(top_low[:, HALF:], jnp.max(high, axis=0, keepdims=True))
    top = jnp.concatenate([top_low[:, :HALF], top_high], axis=1)
    low = jnp.exp2((low - top) * LOG2E)
    high = jnp.exp2((high - top_high) * LOG2E)
    total_low = jnp.sum(low, axis=0, keepdims=True)
    total_high = total_low[:, HALF:] + jnp.sum(high, axis=0, keepdims=True)
    scale_high = 1.0 / total_high
    scale = jnp.concatenate([1.0 / total_low[:, :HALF], scale_high], axis=1)
    return low * scale, high * scale_high


def over_queries(low, high, right):
    first = matmul(low[:, :HALF], right[:HALF], COLS_ROWS)
    second = matmul(jnp.concatenate([low[:, HALF:], high], axis=0), right, COLS_ROWS)
    return jnp.concatenate([first, second], axis=0)


def squares(ref):
    total = None
    for h in range(ref.shape[1] // HD):
        block = ref[:, h * HD : (h + 1) * HD].astype(jnp.float32)
        total = block * block if total is None else total + block * block
    return token_row(total)


def put_rows(out_ref, rows):
    stacked = jnp.concatenate(rows + [jnp.zeros((8 - len(rows), TOK), jnp.float32)], axis=0)
    out_ref[...] = jnp.broadcast_to(stacked[None], out_ref.shape)


def squares_kernel(x_ref, stored_ref, parked_ref, out_ref):
    put_rows(out_ref, [squares(x_ref), squares(stored_ref), squares(parked_ref)])


def forward_kernel(micro, pick, select, len_ref, x_ref, sums_ref, gain_ref, qgain_ref, *rest):
    if select:
        other_ref, y_ref, squares_ref, inv, bias, total = rest
    else:
        y_ref, inv, bias = rest
    if pick is None:
        row = sums_ref[0:1, :]
    else:
        row = gathered_row(sums_ref, pick)
    inv[...] = token_columns(inverse_rms(row))
    fill_bias(bias, len_ref[micro(lax.axis_index("section"))])
    if select:
        total[...] = jnp.zeros_like(total)

    def body(h, carry):
        cols = head_columns(h)
        x = x_ref[:, cols].astype(jnp.float32)
        normed = x * inv[...] * gain_ref[0:1, cols]
        hidden = normed.astype(jnp.bfloat16)
        query = (normed * (qgain_ref[0:1, cols] * (1.0 / HD))).astype(jnp.bfloat16)
        low, high = attention(hidden, query, bias)
        mixed = over_queries(low.astype(jnp.bfloat16), high.astype(jnp.bfloat16), hidden)
        y = (x + mixed).astype(jnp.bfloat16)
        if select:
            y = jnp.where(lax.axis_index("section") == lax.axis_size("section") - 1, other_ref[:, cols], y)
            y_float = y.astype(jnp.float32)
            total[...] += y_float * y_float
        y_ref[:, cols] = y
        return carry

    over_heads(x_ref.shape[1] // HD, body)
    if select:
        squares_ref[...] = jnp.broadcast_to(token_row(total[...]), squares_ref.shape)


def rows_of(refs, cols):
    return jnp.concatenate([r[:, cols].astype(jnp.float32) for r in refs], axis=0)


def backward_kernel(micro, pick, first, parts, len_ref, *rest):
    x_refs, (dy_ref, sums_ref, gain_ref, qgain_ref), rest = rest[:parts], rest[parts : parts + 4], rest[parts + 4 :]
    if first:
        extra_ref, d_unit_ref, sums_out_ref, gain_out, qgain_out, inv, bias, total = rest
    else:
        gain_in, qgain_in, d_unit_ref, sums_out_ref, gain_out, qgain_out, inv, bias, total = rest
    if pick is None:
        row = sums_ref[0:1, :]
    else:
        row = gathered_row(sums_ref, pick)
    inv[...] = token_columns(inverse_rms(row))
    fill_bias(bias, len_ref[micro(lax.axis_index("section"))])
    total[...] = jnp.zeros_like(total)

    def body(h, carry):
        cols = head_columns(h)
        unit = rows_of(x_refs, cols) * inv[...]
        gain = gain_ref[0:1, cols]
        small_qgain = qgain_ref[0:1, cols] * (1.0 / HD)
        normed = unit * gain
        hidden = normed.astype(jnp.bfloat16)
        query = (normed * small_qgain).astype(jnp.bfloat16)
        dy = dy_ref[:, cols]
        low, high = attention(hidden, query, bias)
        d_low = matmul(hidden[:HALF], dy, ROWS_ROWS)
        d_high = matmul(hidden[HALF:], dy[HALF:], ROWS_ROWS)
        mean_low = jnp.sum(low * d_low, axis=0, keepdims=True)
        mean_high = mean_low[:, HALF:] + jnp.sum(high * d_high, axis=0, keepdims=True)
        mean = jnp.concatenate([mean_low[:, :HALF], mean_high], axis=1)
        ds_low = (low * (d_low - mean)).astype(jnp.bfloat16)
        ds_high = (high * (d_high - mean_high)).astype(jnp.bfloat16)
        low = low.astype(jnp.bfloat16)
        high = high.astype(jnp.bfloat16)
        first_keys = matmul(
            jnp.concatenate([ds_low, low], axis=1), jnp.concatenate([query, dy], axis=0), PLAIN
        )
        last_keys = matmul(
            jnp.concatenate([ds_high, high], axis=1),
            jnp.concatenate([query[HALF:], dy[HALF:]], axis=0),
            PLAIN,
        )
        d_query = over_queries(ds_low, ds_high, hidden)
        d_normed = d_query * small_qgain + jnp.concatenate([first_keys, last_keys], axis=0)
        qgain_part = jnp.sum(d_query * normed, axis=0, keepdims=True) * (1.0 / HD)
        along = d_normed * unit
        gain_part = jnp.sum(along, axis=0, keepdims=True)
        if not first:
            qgain_part = qgain_part + qgain_in[0:1, cols]
            gain_part = gain_part + gain_in[0:1, cols]
        qgain_out[0:1, cols] = qgain_part
        gain_out[0:1, cols] = gain_part
        total[...] += along * gain
        d_unit_ref[:, cols] = d_normed * gain
        return carry

    over_heads(dy_ref.shape[1] // HD, body)
    rows = [token_row(total[...])]
    if first:
        rows.append(extra_ref[0:1, :])
    put_rows(sums_out_ref, rows)


def finish_kernel(pick, first, parts, flag_ref, *rest):
    x_refs, (dy_ref, d_unit_ref, sums_ref, project_ref), rest = rest[:parts], rest[parts : parts + 4], rest[parts + 4 :]
    if first:
        other_ref, out_ref, passed_ref, inv, project = rest
    else:
        out_ref, inv, project = rest
    if pick is None:
        row = sums_ref[0:1, :]
    else:
        row = gathered_row(sums_ref, pick)
    inv[...] = token_columns(inverse_rms(row))
    project[...] = token_columns(gathered_row(project_ref, 0) / D)
    for h in range(dy_ref.shape[1] // HD):
        cols = slice(h * HD, (h + 1) * HD)
        unit = rows_of(x_refs, cols) * inv[...]
        dx = dy_ref[:, cols].astype(jnp.float32) + inv[...] * (
            d_unit_ref[:, cols] - unit * project[...]
        )
        dx = dx.astype(jnp.bfloat16)
        if first:
            dx = jnp.where(lax.axis_index("section") == 0, other_ref[:, cols], dx)
        out_ref[:, cols] = dx
    if first:
        passed_ref[...] = jnp.broadcast_to(gathered_row(project_ref, 1), passed_ref.shape)


VMEM = pl.BlockSpec(memory_space=pltpu.VMEM)
SMEM = pl.BlockSpec(memory_space=pltpu.SMEM)


def call(kernel, name, args, outs, scratch, flops, smem_first=True, after=()):
    read = sum(a.size * a.dtype.itemsize for a in args)
    written = sum(o.size * o.dtype.itemsize for o in outs)
    def body(*refs):
        kernel(*refs[: len(args)], *refs[len(args) + len(after) :])

    return pl.pallas_call(
        body,
        name=name,
        out_shape=outs,
        in_specs=[SMEM if (smem_first and i == 0) else VMEM for i in range(len(args))]
        + [pl.BlockSpec(memory_space=pl.ANY)] * len(after),
        out_specs=[VMEM] * len(outs),
        scratch_shapes=scratch,
        compiler_params=pltpu.CompilerParams(vmem_limit_bytes=VMEM_LIMIT),
        cost_estimate=pl.CostEstimate(
            flops=int(flops * COST), bytes_accessed=int((read + written) * COST), transcendentals=0
        ),
    )(*args, *after)


def shape(dims, kind):
    return jax.ShapeDtypeStruct(dims, kind)


SUMS = shape((8, 8, TOK), jnp.float32)
COLS = pltpu.VMEM((TOK, HD), jnp.float32)
BIAS = pltpu.VMEM((TOK, TOK), jnp.float32)


def squares_call(x, stored, parked):
    return call(squares_kernel, "squares", [x, stored, parked], [SUMS], [], 10**9, False)[0]


def forward_first(micro, lens, x, sums, gain, qgain, other, after=()):
    outs = [shape(x.shape, jnp.bfloat16), shape((8, TOK), jnp.float32)]
    return call(
        functools.partial(forward_kernel, micro, 0, True), "forward_first",
        [lens, x, sums, gain, qgain, other], outs, [COLS, BIAS, COLS], 3 * 10**9, True, after,
    )


def forward_second(micro, lens, x, sums, gain, qgain, after=()):
    return call(
        functools.partial(forward_kernel, micro, None, False), "forward_second",
        [lens, x, sums, gain, qgain], [shape(x.shape, jnp.bfloat16)], [COLS, BIAS], 3 * 10**9, True, after,
    )[0]


def backward_call(micro, first, lens, x, dy, sums, gain, qgain, rest, after=()):
    outs = [shape(dy.shape, jnp.float32), SUMS, shape(gain.shape, jnp.float32), shape(gain.shape, jnp.float32)]
    return call(
        functools.partial(backward_kernel, micro, 1 if first else None, first, len(x)),
        "backward_first" if first else "backward_second",
        [lens, *x, dy, sums, gain, qgain] + rest, outs, [COLS, BIAS, COLS], 6 * 10**9, True, after,
    )


def finish_call(first, lens, x, dy, d_unit, sums, project, rest, after=()):
    outs = [shape(dy.shape, jnp.bfloat16)]
    if first:
        outs.append(shape((8, TOK), jnp.float32))
    return call(
        functools.partial(finish_kernel, 1 if first else None, first, len(x)),
        "finish_first" if first else "finish_second",
        [lens, *x, dy, d_unit, sums, project] + rest, outs, [COLS, COLS], 10**9, True, after,
    )


def settle_kernel(*refs):
    pass


def settle(parts, after):
    whole = parts[0]
    in_hbm = pl.BlockSpec(memory_space=pltpu.HBM)
    return pl.pallas_call(
        settle_kernel,
        name="settle",
        out_shape=shape(whole.shape, whole.dtype),
        in_specs=[in_hbm] + [pl.BlockSpec(memory_space=pl.ANY)] * len(after),
        out_specs=in_hbm,
        input_output_aliases={0: 0},
    )(whole, *after)


def gathered(sums):
    return lax.all_to_all(sums, "tensor", 0, 0)


def per_device(x_in, grad_in, stash_near, parked_in, fresh, loss_grad, gain, qgain, lengths):
    count = lax.axis_size("section")
    mirrored = [(i, count - 1 - i) for i in range(count)]
    parking = [(i, (count - 2 - i) % count) for i in range(count)]
    onward = [(i, (i + 1) % count) for i in range(count)]
    back = [((i + 1) % count, i) for i in range(count)]
    x, dy, stored, parked = x_in[0], grad_in[0], stash_near[0], parked_in[0]
    fetched = []
    at = 0
    for rows_n in MIRROR_ROWS:
        fetched.append(lax.ppermute(parked[at : at + rows_n], "section", mirrored))
        at += rows_n
    made = {f"m{i}": v for i, v in enumerate(fetched)}

    def after(k):
        return [made[n] for n in AFTER[k]]

    sums = gathered(squares_call(x, stored, parked))
    stored_squares = jnp.sum(sums[:, 2, :], axis=0, keepdims=True)
    stored_squares = lax.ppermute(jnp.broadcast_to(stored_squares, (8, TOK)), "section", mirrored)
    made["tm"] = stored_squares
    first_out, first_squares = forward_first(
        lambda s: 2 * count - 1 - s, lengths, x, sums, gain, qgain, fresh, after(0)
    )
    x_two = lax.ppermute(first_out, "section", onward)
    parked_out = []
    at = 0
    for i, rows_n in enumerate(PARK_ROWS):
        parked_out.append(lax.ppermute(first_out[at : at + rows_n], "section", parking))
        made[f"p{i}"] = parked_out[-1]
        at += rows_n
    made["x"] = x_two
    d_unit, project, gain_one, qgain_one = backward_call(
        lambda s: s, True, lengths, [stored], dy, sums, gain, qgain, [first_squares], after(1)
    )
    project = gathered(project)
    first_grad, passed = finish_call(
        True, lengths, [stored], dy, d_unit, sums, project, [loss_grad], after(2)
    )
    d_two = lax.ppermute(first_grad, "section", back)
    two_squares = lax.ppermute(passed, "section", onward)
    second_out = forward_second(
        lambda s: 2 * count - s, lengths, x_two, two_squares, gain, qgain, after(4)
    )
    d_unit, project, gain_two, qgain_two = backward_call(
        lambda s: s + 1, False, lengths, fetched, d_two, stored_squares, gain, qgain, [gain_one, qgain_one], after(3)
    )
    project = gathered(project)
    second_grad = finish_call(False, lengths, fetched, d_two, d_unit, stored_squares, project, [], after(5))[0]
    parked_out = settle(parked_out, [made[n] for n in AFTER[6]] + ([second_grad] if LAST else []))
    return (
        second_out[None],
        second_grad[None],
        parked_out[None],
        gain_two,
        qgain_two,
    )


def solution(mesh):
    wide = P("section", None, "tensor")
    narrow = P(None, "tensor")
    rows = P("section", "tensor")
    return jax.shard_map(
        per_device,
        mesh=mesh,
        in_specs=(wide, wide, wide, wide, narrow, narrow, rows, rows, P()),
        out_specs=(wide, wide, wide, rows, rows),
        check_vma=False,
    )
```

time: 319 us -> 116 us (0.36)
  the two profiles are of different devices: /device:TPU:1 before, /device:TPU:2 now
where the time goes in v1:
time: 116 us; the launch traced here: 115 us
  waiting for transfers between devices  46.7 us (40%)
  starting transfers between devices  31.3 us (27%)
  Pallas kernels  27.4 us (24%)
  local copies, waits for them, and re-layouts  8.88 us (8%)
    pallas_call x7, Pallas kernels, call(): pl.pallas_call(body, name=name, out_shape=outs, in_specs=[SMEM if smem_fi...  27.4 us
    ppermute x1, waiting for transfers between devices, per_device(): d_two = lax.ppermute(first_grad, 'section', back)  24.2 us
    ppermute x1, waiting for transfers between devices, per_device(): lax.ppermute(jnp.broadcast_to(stored_squares, (8, TOK)), 'section', mirro...  20.9 us
    all_to_all x3, starting transfers between devices, gathered(): return lax.all_to_all(sums, 'tensor', 0, 0)  17.5 us
    unnamed x25, local copies, waits for them, and re-layouts  8.88 us
    ppermute x1, starting transfers between devices, per_device(): fetched.append(lax.ppermute(parked[at:at + rows_n], 'section', mirrored))  6.3 us
    ppermute x1, starting transfers between devices, per_device(): lax.ppermute(jnp.broadcast_to(stored_squares, (8, TOK)), 'section', mirro...  3.65 us
  transfers between devices with their start and end apart: 9, of which 3 were waited for; matrix products, arithmetic and copies ran while one was open for 0% of the time, Pallas kernels for 22%

profile of v1, /device:TPU:2, one launch (start us, length us, event | category | flops | bytes accessed | tf_op | source)
XLA Modules:
  0.0 115.0 jit_solution(9605498768730645722)
XLA Ops:
  0.6 0.0 copy-start
  0.6 1.1 copy-done
  1.8 0.0 copy-start.6
  1.8 1.1 copy-done.6
  2.9 0.0 copy-start.9
  2.9 1.1 copy-done.9
  4.0 0.0 copy-start.5
  4.0 0.0 copy-start.7
  4.0 0.0 copy-start.8
  4.0 0.0 copy-start.10
  4.0 0.0 copy-start.11
  4.1 1.2 %squares.1 = f32[8,8,256]{2,1,0:T(8,128)} custom-call(bf16[256,1536]{1,0:T(8,128)(2,1)S(1)} %bitcast.12, bf16[256,1536]{1,0:T(8,128)(2,1)S(1)} %bitcast.7, bf16[256,1536]{1,0:T(8,128)(2,1)S(1)} %bitcast.15), custom_call_target="tpu_custom_call" | custom-call | flops 1000000000 | bytes 2424832 | tf_op jit(solution)/shard_map/squares/pallas_call | solution.py:244
  5.2 5.9 %all-to-all-start = ((f32[8,8,256]{2,1,0:T(8,128)}), f32[8,8,256]{2,1,0:T(8,128)S(1)}, u32[]{:S(2)}, u32[]{:S(2)}) async-start(f32[8,8,256]{2,1,0:T(8,128)} %squares.1), calls=%async_computation | async-start | bytes 131072 | tf_op jit(solution)/shard_map/all_to_all | solution.py:325
  11.1 0.0 copy-start.1
  11.1 6.3 %collective-permute-start.1 = (bf16[256,1536]{1,0:T(8,128)(2,1)}, bf16[256,1536]{1,0:T(8,128)(2,1)S(1)}, u32[]{:S(2)}, u32[]{:S(2)}) collective-permute-start(bf16[256,1536]{1,0:T(8,128)(2,1)} %bitcast.14), channel_id=1, source_target_pairs={{0,248},{8,240},{16,232},{24,224},{32,216},{40,208},{48,200},{56,1... | collective-permute-start | bytes 2359304 | tf_op jit(solution)/shard_map/ppermute | solution.py:338
  17.4 0.0 all-to-all-done.refs_2_.refs_3_.refs_4_
  17.4 0.0 copy-done.5
  17.4 0.0 copy-done.7
  17.5 0.0 copy-done.8
  17.5 0.0 copy-done.10
  17.5 0.0 copy-done.11
  17.5 5.5 %forward_first.1 = (bf16[256,1536]{1,0:T(8,128)(2,1)}, f32[8,256]{1,0:T(8,128)S(1)}) custom-call(s32[65]{0:T(128)S(1)} %copy-done.5, bf16[256,1536]{1,0:T(8,128)(2,1)S(1)} %bitcast.13, f32[8,8,256]{2,1,0:T(8,128)S(1)} %all-to-all-done.refs_2_.refs_3_.refs_4_, f32[1,1536]{1,0:T(1,128)S(1)} %copy-done.10, f32[1,1536]{1,0:T(1,128)S(1)} %copy-done.11, ...), custom_call_target="tpu_custom_call" | custom-call | flops 3000000000 | bytes 2445572 | tf_op jit(solution)/shard_map/forward_first/pallas_call | solution.py:244
  23.0 1.2 %collective-permute-start = (bf16[256,1536]{1,0:T(8,128)(2,1)}, bf16[256,1536]{1,0:T(8,128)(2,1)}, u32[]{:S(2)}, u32[]{:S(2)}) collective-permute-start(bf16[256,1536]{1,0:T(8,128)(2,1)} %get-tuple-element.17), channel_id=1, source_target_pairs={{0,8},{8,16},{16,24},{24,32},{32,40},{40,48},{48,56},{56,64},{64,7... | collective-permute-start | bytes 2359304 | tf_op jit(solution)/shard_map/ppermute | solution.py:352
  24.2 0.0 copy-done.1
  24.3 0.0 copy-start.2
  24.3 1.1 copy-done.2
  25.4 5.8 %backward_first.1 = (f32[256,1536]{1,0:T(8,128)S(1)}, f32[8,8,256]{2,1,0:T(8,128)}, f32[1,1536]{1,0:T(1,128)S(1)}, f32[1,1536]{1,0:T(1,128)S(1)}) custom-call(s32[65]{0:T(128)S(1)} %copy-done.5, bf16[256,1536]{1,0:T(8,128)(2,1)S(1)} %bitcast.8, bf16[256,1536]{1,0:T(8,128)(2,1)S(1)} %bitcast.10, f32[8,8,256]{2,1,0:T(8,128)S(1)} %all-to-all-done.refs_2_.refs_3_.refs_4_, ...), custom_call_target="tpu_custom_call" | custom-call | flops 6000000000 | bytes 3309828 | tf_op jit(solution)/shard_map/backward_first/pallas_call | solution.py:244
  31.2 5.7 %all-to-all-start.1 = ((f32[8,8,256]{2,1,0:T(8,128)}), f32[8,8,256]{2,1,0:T(8,128)S(1)}, u32[]{:S(2)}, u32[]{:S(2)}) async-start(f32[8,8,256]{2,1,0:T(8,128)} %get-tuple-element.20), calls=%async_computation.1 | async-start | bytes 131072 | tf_op jit(solution)/shard_map/all_to_all | solution.py:325
  36.9 3.7 %collective-permute-start.2 = (f32[8,256]{1,0:T(8,128)S(1)}, f32[8,256]{1,0:T(8,128)S(1)}, u32[]{:S(2)}, u32[]{:S(2)}) collective-permute-start(f32[8,256]{1,0:T(8,128)S(1)} %broadcast_in_dim.15), channel_id=1, source_target_pairs={{0,248},{8,240},{16,232},{24,224},{32,216},{40,208},{48,200},{56,1... | collective-permute-start | bytes 24584 | tf_op jit(solution)/shard_map/ppermute | solution.py:347
  40.6 20.9 %collective-permute-done.2.refs_8_.refs_3_.refs_4_ = f32[8,256]{1,0:T(8,128)S(1)} collective-permute-done((f32[8,256]{1,0:T(8,128)S(1)}, f32[8,256]{1,0:T(8,128)S(1)}, u32[]{:S(2)}, u32[]{:S(2)}) %collective-permute-start.2) | collective-permute-done | bytes 8224 | tf_op jit(solution)/shard_map/ppermute | solution.py:347
  61.4 1.6 %all-to-all-done.1.refs_5_ = f32[8,8,256]{2,1,0:T(8,128)S(1)} async-done(((f32[8,8,256]{2,1,0:T(8,128)}), f32[8,8,256]{2,1,0:T(8,128)S(1)}, u32[]{:S(2)}, u32[]{:S(2)}) %all-to-all-start.1) | async-done | bytes 65568 | tf_op jit(solution)/shard_map/all_to_all | solution.py:325
  63.0 0.0 collective-permute-done.1.refs_7_.refs_1_
  63.0 0.0 collective-permute-done.refs_9_.refs_1_
  63.0 0.0 copy-start.3
  63.0 1.1 copy-done.3
  64.1 0.0 copy-start.4
  64.1 1.1 copy-done.4
  65.3 1.1 finish_first.1
  66.4 0.1 collective-permute-start.4
  66.5 1.9 %collective-permute-start.5 = (bf16[256,1536]{1,0:T(8,128)(2,1)}, bf16[256,1536]{1,0:T(8,128)(2,1)}, u32[]{:S(2)}, u32[]{:S(2)}) collective-permute-start(bf16[256,1536]{1,0:T(8,128)(2,1)} %get-tuple-element.17), channel_id=1, source_target_pairs={{0,240},{8,232},{16,224},{24,216},{32,208},{40,200},{48,192},{56,1... | collective-permute-start | bytes 2359304 | tf_op jit(solution)/shard_map/ppermute | solution.py:356
  68.4 0.6 collective-permute-start.3
  69.0 24.2 %collective-permute-done.4.refs_2_ = bf16[256,1536]{1,0:T(8,128)(2,1)S(1)} collective-permute-done((bf16[256,1536]{1,0:T(8,128)(2,1)S(1)}, bf16[256,1536]{1,0:T(8,128)(2,1)S(1)}, u32[]{:S(2)}, u32[]{:S(2)}) %collective-permute-start.4) | collective-permute-done | bytes 786464 | tf_op jit(solution)/shard_map/ppermute | solution.py:367
  93.2 5.7 %backward_second.1 = (f32[256,1536]{1,0:T(8,128)S(1)}, f32[8,8,256]{2,1,0:T(8,128)}, f32[1,1536]{1,0:T(1,128)}, f32[1,1536]{1,0:T(1,128)}) custom-call(s32[65]{0:T(128)S(1)} %copy-done.5, bf16[256,1536]{1,0:T(8,128)(2,1)S(1)} %collective-permute-done.1.refs_7_.refs_1_, bf16[256,1536]{1,0:T(8,128)(2,1)S(1)} %collective-permute-done.4.refs_2_, ...), custom_call_target="tpu_custom_call" | custom-call | flops 6000000000 | bytes 3256580 | tf_op jit(solution)/shard_map/backward_second/pallas_call | solution.py:244
  98.9 5.9 %all-to-all-start.2 = ((f32[8,8,256]{2,1,0:T(8,128)}), f32[8,8,256]{2,1,0:T(8,128)S(1)}, u32[]{:S(2)}, u32[]{:S(2)}) async-start(f32[8,8,256]{2,1,0:T(8,128)} %get-tuple-element.26), calls=%async_computation.2 | async-start | bytes 131072 | tf_op jit(solution)/shard_map/all_to_all | solution.py:325
  104.8 0.0 collective-permute-done.3.refs_2_
  104.9 6.1 %forward_second.1 = bf16[256,1536]{1,0:T(8,128)(2,1)} custom-call(s32[65]{0:T(128)S(1)} %copy-done.5, bf16[256,1536]{1,0:T(8,128)(2,1)} %collective-permute-done.refs_9_.refs_1_, f32[8,256]{1,0:T(8,128)S(1)} %collective-permute-done.3.refs_2_, f32[1,1536]{1,0:T(1,128)S(1)} %copy-done.10, f32[1,1536]{1,0:T(1,128)S(1)} %copy-done.11), custom_call_target="tpu_custom_call" | custom-call | flops 3000000000 | bytes 1593604 | tf_op jit(solution)/shard_map/forward_second/pallas_call | solution.py:244
  110.9 0.0 all-to-all-done.2.refs_5_
  110.9 1.9 %finish_second.1.refs_1_ = bf16[256,1536]{1,0:T(8,128)(2,1)} custom-call(s32[65]{0:T(128)S(1)} %copy-done.5, bf16[256,1536]{1,0:T(8,128)(2,1)S(1)} %collective-permute-done.1.refs_7_.refs_1_, bf16[256,1536]{1,0:T(8,128)(2,1)S(1)} %collective-permute-done.4.refs_2_, f32[256,1536]{1,0:T(8,128)S(1)} %get-tuple-element.25.refs_3_, ...), custom_call_target="tpu_custom_call" | custom-call | flops 1000000000 | bytes 4006148 | tf_op jit(solution)/shard_map/finish_second/pallas_call | solution.py:244
  112.9 0.0 collective-permute-done.5.refs_0_
  112.9 2.1 %copy.17 = bf16[1,256,1536]{2,1,0:T(8,128)(2,1)} copy(bf16[1,256,1536]{2,1,0:T(8,128)(2,1)} %bitcast.6) | data formatting | bytes 1572864
  (3 shorter events, 0.0 us)
Async XLA Ops:
  0.6 1.1 copy-start
  1.8 1.1 copy-start.6
  2.9 1.1 copy-start.9
  4.0 13.4 %copy-start.5 = (s32[65]{0:T(128)S(1)}, s32[65]{0:T(128)}, u32[]{:S(2)}) copy-start(s32[65]{0:T(128)} %refs_0_.11) | copy-start | bytes 784
  4.0 13.4 %copy-start.7 = (bf16[1,256,1536]{2,1,0:T(8,128)(2,1)S(1)}, bf16[1,256,1536]{2,1,0:T(8,128)(2,1)}, u32[]{:S(2)}) copy-start(bf16[1,256,1536]{2,1,0:T(8,128)(2,1)} %param.9) | copy-start | bytes 2359300
  4.0 13.4 %copy-start.8 = (bf16[256,1536]{1,0:T(8,128)(2,1)S(1)}, bf16[256,1536]{1,0:T(8,128)(2,1)}, u32[]{:S(2)}) copy-start(bf16[256,1536]{1,0:T(8,128)(2,1)} %refs_5_.3) | copy-start | bytes 2359300
  4.0 13.4 %copy-start.10 = (f32[1,1536]{1,0:T(1,128)S(1)}, f32[1,1536]{1,0:T(1,128)}, u32[]{:S(2)}) copy-start(f32[1,1536]{1,0:T(1,128)} %refs_4_.7) | copy-start | bytes 18436
  4.0 13.4 %copy-start.11 = (f32[1,1536]{1,0:T(1,128)S(1)}, f32[1,1536]{1,0:T(1,128)}, u32[]{:S(2)}) copy-start(f32[1,1536]{1,0:T(1,128)} %refs_5_.5) | copy-start | bytes 18436
  5.2 12.2 %all-to-all-start = ((f32[8,8,256]{2,1,0:T(8,128)}), f32[8,8,256]{2,1,0:T(8,128)S(1)}, u32[]{:S(2)}, u32[]{:S(2)}) async-start(f32[8,8,256]{2,1,0:T(8,128)} %squares.1), calls=%async_computation | async-start | bytes 131072 | tf_op jit(solution)/shard_map/all_to_all | solution.py:325
  11.1 13.1 %copy-start.1 = (bf16[1,256,1536]{2,1,0:T(8,128)(2,1)S(1)}, bf16[1,256,1536]{2,1,0:T(8,128)(2,1)}, u32[]{:S(2)}) copy-start(bf16[1,256,1536]{2,1,0:T(8,128)(2,1)} %param.11) | copy-start | bytes 2359300
  11.1 51.9 %collective-permute-start.1 = (bf16[256,1536]{1,0:T(8,128)(2,1)}, bf16[256,1536]{1,0:T(8,128)(2,1)S(1)}, u32[]{:S(2)}, u32[]{:S(2)}) collective-permute-start(bf16[256,1536]{1,0:T(8,128)(2,1)} %bitcast.14), channel_id=1, source_target_pairs={{0,248},{8,240},{16,232},{24,224},{32,216},{40,208},{48,200},{56,1... | collective-permute-start | bytes 2359304 | tf_op jit(solution)/shard_map/ppermute | solution.py:338
  23.0 40.0 %collective-permute-start = (bf16[256,1536]{1,0:T(8,128)(2,1)}, bf16[256,1536]{1,0:T(8,128)(2,1)}, u32[]{:S(2)}, u32[]{:S(2)}) collective-permute-start(bf16[256,1536]{1,0:T(8,128)(2,1)} %get-tuple-element.17), channel_id=1, source_target_pairs={{0,8},{8,16},{16,24},{24,32},{32,40},{40,48},{48,56},{56,64},{64,7... | collective-permute-start | bytes 2359304 | tf_op jit(solution)/shard_map/ppermute | solution.py:352
  24.3 1.1 copy-start.2
  31.2 31.8 %all-to-all-start.1 = ((f32[8,8,256]{2,1,0:T(8,128)}), f32[8,8,256]{2,1,0:T(8,128)S(1)}, u32[]{:S(2)}, u32[]{:S(2)}) async-start(f32[8,8,256]{2,1,0:T(8,128)} %get-tuple-element.20), calls=%async_computation.1 | async-start | bytes 131072 | tf_op jit(solution)/shard_map/all_to_all | solution.py:325
  36.9 24.5 %collective-permute-start.2 = (f32[8,256]{1,0:T(8,128)S(1)}, f32[8,256]{1,0:T(8,128)S(1)}, u32[]{:S(2)}, u32[]{:S(2)}) collective-permute-start(f32[8,256]{1,0:T(8,128)S(1)} %broadcast_in_dim.15), channel_id=1, source_target_pairs={{0,248},{8,240},{16,232},{24,224},{32,216},{40,208},{48,200},{56,1... | collective-permute-start | bytes 24584 | tf_op jit(solution)/shard_map/ppermute | solution.py:347
  63.0 1.1 copy-start.3
  64.1 1.1 copy-start.4
  66.4 26.8 %collective-permute-start.4 = (bf16[256,1536]{1,0:T(8,128)(2,1)S(1)}, bf16[256,1536]{1,0:T(8,128)(2,1)S(1)}, u32[]{:S(2)}, u32[]{:S(2)}) collective-permute-start(bf16[256,1536]{1,0:T(8,128)(2,1)S(1)} %get-tuple-element.22), channel_id=1, source_target_pairs={{8,0},{16,8},{24,16},{32,24},{40,32},{48,40},{56,48},{64,56},{72,6... | collective-permute-start | bytes 2359304 | tf_op jit(solution)/shard_map/ppermute | solution.py:367
  66.5 46.4 %collective-permute-start.5 = (bf16[256,1536]{1,0:T(8,128)(2,1)}, bf16[256,1536]{1,0:T(8,128)(2,1)}, u32[]{:S(2)}, u32[]{:S(2)}) collective-permute-start(bf16[256,1536]{1,0:T(8,128)(2,1)} %get-tuple-element.17), channel_id=1, source_target_pairs={{0,240},{8,232},{16,224},{24,216},{32,208},{40,200},{48,192},{56,1... | collective-permute-start | bytes 2359304 | tf_op jit(solution)/shard_map/ppermute | solution.py:356
  68.4 36.4 %collective-permute-start.3 = (f32[8,256]{1,0:T(8,128)S(1)}, f32[8,256]{1,0:T(8,128)S(1)}, u32[]{:S(2)}, u32[]{:S(2)}) collective-permute-start(f32[8,256]{1,0:T(8,128)S(1)} %get-tuple-element.21), channel_id=1, source_target_pairs={{0,8},{8,16},{16,24},{24,32},{32,40},{40,48},{48,56},{56,64},{64,7... | collective-permute-start | bytes 24584 | tf_op jit(solution)/shard_map/ppermute | solution.py:368
  98.9 12.0 %all-to-all-start.2 = ((f32[8,8,256]{2,1,0:T(8,128)}), f32[8,8,256]{2,1,0:T(8,128)S(1)}, u32[]{:S(2)}, u32[]{:S(2)}) async-start(f32[8,8,256]{2,1,0:T(8,128)} %get-tuple-element.26), calls=%async_computation.2 | async-start | bytes 131072 | tf_op jit(solution)/shard_map/all_to_all | solution.py:325

commit v2 on v1

--- a/solution.py
+++ b/solution.py
@@ -15,12 +15,12 @@
 LOG2E = 1.4426950408889634
 MASKED = -1e30
 VMEM_LIMIT = 40 * 1024 * 1024
+WHOLE_VMEM = 62 * 1024 * 1024
 UNROLL = 6
 COST = 1.0
-MIRROR_ROWS = (256,)
-AFTER = ((), (), ('m0', 'tm', 'x', ), (), (), (), ())
-PARK_ROWS = (256,)
+AFTER = ((), (), (), ('m', 'tm', ), (), (), ())
 LAST = True
+HOLD = True
 
 ROWS_ROWS = (((1,), (1,)), ((), ()))
 COLS_ROWS = (((0,), (0,)), ((), ()))
@@ -100,13 +100,21 @@
     out_ref[...] = jnp.broadcast_to(stacked[None], out_ref.shape)
 
 
-def squares_kernel(x_ref, stored_ref, parked_ref, out_ref):
-    put_rows(out_ref, [squares(x_ref), squares(stored_ref), squares(parked_ref)])
+def squares_kernel(x_ref, stored_ref, parked_ref, out_ref, held, arrived):
+    refs = (x_ref, stored_ref, parked_ref)
+    copies = [pltpu.make_async_copy(r, held.at[k], arrived.at[k]) for k, r in enumerate(refs)]
+    for copy in copies:
+        copy.start()
+    rows = []
+    for k, copy in enumerate(copies):
+        copy.wait()
+        rows.append(squares(held.at[k]))
+    put_rows(out_ref, rows)
 
 
 def forward_kernel(micro, pick, select, len_ref, x_ref, sums_ref, gain_ref, qgain_ref, *rest):
     if select:
-        other_ref, y_ref, squares_ref, inv, bias, total = rest
+        other_ref, y_ref, copy_ref, inv, bias = rest
     else:
         y_ref, inv, bias = rest
     if pick is None:
@@ -115,9 +123,6 @@
         row = gathered_row(sums_ref, pick)
     inv[...] = token_columns(inverse_rms(row))
     fill_bias(bias, len_ref[micro(lax.axis_index("section"))])
-    if select:
-        total[...] = jnp.zeros_like(total)
-
     def body(h, carry):
         cols = head_columns(h)
         x = x_ref[:, cols].astype(jnp.float32)
@@ -129,14 +134,12 @@
         y = (x + mixed).astype(jnp.bfloat16)
         if select:
             y = jnp.where(lax.axis_index("section") == lax.axis_size("section") - 1, other_ref[:, cols], y)
-            y_float = y.astype(jnp.float32)
-            total[...] += y_float * y_float
         y_ref[:, cols] = y
+        if select:
+            copy_ref[:, cols] = y
         return carry
 
     over_heads(x_ref.shape[1] // HD, body)
-    if select:
-        squares_ref[...] = jnp.broadcast_to(token_row(total[...]), squares_ref.shape)
 
 
 def rows_of(refs, cols):
@@ -146,9 +149,9 @@
 def backward_kernel(micro, pick, first, parts, len_ref, *rest):
     x_refs, (dy_ref, sums_ref, gain_ref, qgain_ref), rest = rest[:parts], rest[parts : parts + 4], rest[parts + 4 :]
     if first:
-        extra_ref, d_unit_ref, sums_out_ref, gain_out, qgain_out, inv, bias, total = rest
-    else:
-        gain_in, qgain_in, d_unit_ref, sums_out_ref, gain_out, qgain_out, inv, bias, total = rest
+        d_unit_ref, sums_out_ref, gain_out, qgain_out, inv, bias, total = rest
+    else:
+        gain_in, qgain_in, next_ref, d_unit_ref, sums_out_ref, gain_out, qgain_out, inv, bias, total = rest
     if pick is None:
         row = sums_ref[0:1, :]
     else:
@@ -200,15 +203,15 @@
 
     over_heads(dy_ref.shape[1] // HD, body)
     rows = [token_row(total[...])]
-    if first:
-        rows.append(extra_ref[0:1, :])
+    if not first:
+        rows.append(squares(next_ref))
     put_rows(sums_out_ref, rows)
 
 
 def finish_kernel(pick, first, parts, flag_ref, *rest):
     x_refs, (dy_ref, d_unit_ref, sums_ref, project_ref), rest = rest[:parts], rest[parts : parts + 4], rest[parts + 4 :]
     if first:
-        other_ref, out_ref, passed_ref, inv, project = rest
+        other_ref, out_ref, inv, project = rest
     else:
         out_ref, inv, project = rest
     if pick is None:
@@ -227,8 +230,6 @@
         if first:
             dx = jnp.where(lax.axis_index("section") == 0, other_ref[:, cols], dx)
         out_ref[:, cols] = dx
-    if first:
-        passed_ref[...] = jnp.broadcast_to(gathered_row(project_ref, 1), passed_ref.shape)
 
 
 VMEM = pl.BlockSpec(memory_space=pltpu.VMEM)
@@ -266,20 +267,28 @@
 
 
 def squares_call(x, stored, parked):
-    return call(squares_kernel, "squares", [x, stored, parked], [SUMS], [], 10**9, False)[0]
+    return pl.pallas_call(
+        squares_kernel,
+        name="squares",
+        out_shape=SUMS,
+        in_specs=[pl.BlockSpec(memory_space=pltpu.HBM)] * 3,
+        out_specs=VMEM,
+        scratch_shapes=[pltpu.VMEM((3, *x.shape), x.dtype), pltpu.SemaphoreType.DMA((3,))],
+        compiler_params=pltpu.CompilerParams(vmem_limit_bytes=WHOLE_VMEM),
+    )(x, stored, parked)
 
 
 def forward_first(micro, lens, x, sums, gain, qgain, other, after=()):
-    outs = [shape(x.shape, jnp.bfloat16), shape((8, TOK), jnp.float32)]
+    outs = [shape(x.shape, jnp.bfloat16)] * 2
     return call(
         functools.partial(forward_kernel, micro, 0, True), "forward_first",
-        [lens, x, sums, gain, qgain, other], outs, [COLS, BIAS, COLS], 3 * 10**9, True, after,
+        [lens, x, sums, gain, qgain, other], outs, [COLS, BIAS], 3 * 10**9, True, after,
     )
 
 
 def forward_second(micro, lens, x, sums, gain, qgain, after=()):
     return call(
-        functools.partial(forward_kernel, micro, None, False), "forward_second",
+        functools.partial(forward_kernel, micro, 1, False), "forward_second",
         [lens, x, sums, gain, qgain], [shape(x.shape, jnp.bfloat16)], [COLS, BIAS], 3 * 10**9, True, after,
     )[0]
 
@@ -295,8 +304,6 @@
 
 def finish_call(first, lens, x, dy, d_unit, sums, project, rest, after=()):
     outs = [shape(dy.shape, jnp.bfloat16)]
-    if first:
-        outs.append(shape((8, TOK), jnp.float32))
     return call(
         functools.partial(finish_kernel, 1 if first else None, first, len(x)),
         "finish_first" if first else "finish_second",
@@ -304,21 +311,45 @@
     )
 
 
-def settle_kernel(*refs):
+def settle_kernel(parts, *refs):
+    sources, out, done = refs[:parts], refs[-2], refs[-1]
+    copies = []
+    at = 0
+    for k, source in enumerate(sources):
+        rows_n = source.shape[0]
+        copies.append(pltpu.make_async_copy(source, out.at[pl.ds(at, rows_n), :], done.at[k]))
+        at += rows_n
+    for copy in copies:
+        copy.start()
+    for copy in copies:
+        copy.wait()
+
+
+def settle(parts, after):
+    rows_n = sum(part.shape[0] for part in parts)
+    return pl.pallas_call(
+        functools.partial(settle_kernel, len(parts)),
+        name="settle",
+        out_shape=shape((rows_n, parts[0].shape[1]), parts[0].dtype),
+        in_specs=[VMEM] * len(parts) + [pl.BlockSpec(memory_space=pl.ANY)] * len(after),
+        out_specs=pl.BlockSpec(memory_space=pltpu.HBM),
+        scratch_shapes=[pltpu.SemaphoreType.DMA((len(parts),))],
+    )(*parts, *after)
+
+
+def hold_kernel(*refs):
     pass
 
 
-def settle(parts, after):
-    whole = parts[0]
-    in_hbm = pl.BlockSpec(memory_space=pltpu.HBM)
+def hold(value, after):
     return pl.pallas_call(
-        settle_kernel,
-        name="settle",
-        out_shape=shape(whole.shape, whole.dtype),
-        in_specs=[in_hbm] + [pl.BlockSpec(memory_space=pl.ANY)] * len(after),
-        out_specs=in_hbm,
+        hold_kernel,
+        name="hold",
+        out_shape=shape(value.shape, value.dtype),
+        in_specs=[pl.BlockSpec(memory_space=pl.ANY)] * (1 + len(after)),
+        out_specs=pl.BlockSpec(memory_space=pl.ANY),
         input_output_aliases={0: 0},
-    )(whole, *after)
+    )(value, *after)
 
 
 def gathered(sums):
@@ -332,12 +363,8 @@
     onward = [(i, (i + 1) % count) for i in range(count)]
     back = [((i + 1) % count, i) for i in range(count)]
     x, dy, stored, parked = x_in[0], grad_in[0], stash_near[0], parked_in[0]
-    fetched = []
-    at = 0
-    for rows_n in MIRROR_ROWS:
-        fetched.append(lax.ppermute(parked[at : at + rows_n], "section", mirrored))
-        at += rows_n
-    made = {f"m{i}": v for i, v in enumerate(fetched)}
+    fetched = [lax.ppermute(parked, "section", mirrored)]
+    made = {"m": fetched[0]}
 
     def after(k):
         return [made[n] for n in AFTER[k]]
@@ -346,35 +373,38 @@
     stored_squares = jnp.sum(sums[:, 2, :], axis=0, keepdims=True)
     stored_squares = lax.ppermute(jnp.broadcast_to(stored_squares, (8, TOK)), "section", mirrored)
     made["tm"] = stored_squares
-    first_out, first_squares = forward_first(
-        lambda s: 2 * count - 1 - s, lengths, x, sums, gain, qgain, fresh, after(0)
-    )
+    d_unit, project, gain_one, qgain_one = backward_call(
+        lambda s: s, True, lengths, [stored], dy, sums, gain, qgain, [], after(0)
+    )
+    project = gathered(project)
+    made["a1"] = project
+    first_grad = finish_call(
+        True, lengths, [stored], dy, d_unit, sums, project, [loss_grad], after(1)
+    )[0]
+    made["g1"] = first_grad
+    d_two = lax.ppermute(first_grad, "section", back)
+    made["dx"] = d_two
+    first_out, parking_out = forward_first(
+        lambda s: 2 * count - 1 - s, lengths, x, sums, gain, qgain, fresh, after(2)
+    )
+    if HOLD:
+        parking_out = hold(parking_out, after(3))
+    made["y1"] = first_out
     x_two = lax.ppermute(first_out, "section", onward)
-    parked_out = []
-    at = 0
-    for i, rows_n in enumerate(PARK_ROWS):
-        parked_out.append(lax.ppermute(first_out[at : at + rows_n], "section", parking))
-        made[f"p{i}"] = parked_out[-1]
-        at += rows_n
     made["x"] = x_two
-    d_unit, project, gain_one, qgain_one = backward_call(
-        lambda s: s, True, lengths, [stored], dy, sums, gain, qgain, [first_squares], after(1)
+    parked_out = [lax.ppermute(parking_out, "section", parking)]
+    d_unit, project, gain_two, qgain_two = backward_call(
+        lambda s: s + 1, False, lengths, fetched, d_two, stored_squares, gain, qgain,
+        [gain_one, qgain_one, x_two], after(4),
     )
     project = gathered(project)
-    first_grad, passed = finish_call(
-        True, lengths, [stored], dy, d_unit, sums, project, [loss_grad], after(2)
-    )
-    d_two = lax.ppermute(first_grad, "section", back)
-    two_squares = lax.ppermute(passed, "section", onward)
+    second_grad = finish_call(
+        False, lengths, fetched, d_two, d_unit, stored_squares, project, [], after(5)
+    )[0]
     second_out = forward_second(
-        lambda s: 2 * count - s, lengths, x_two, two_squares, gain, qgain, after(4)
-    )
-    d_unit, project, gain_two, qgain_two = backward_call(
-        lambda s: s + 1, False, lengths, fetched, d_two, stored_squares, gain, qgain, [gain_one, qgain_one], after(3)
-    )
-    project = gathered(project)
-    second_grad = finish_call(False, lengths, fetched, d_two, d_unit, stored_squares, project, [], after(5))[0]
-    parked_out = settle(parked_out, [made[n] for n in AFTER[6]] + ([second_grad] if LAST else []))
+        lambda s: 2 * count - s, lengths, x_two, project, gain, qgain, after(6)
+    )
+    parked_out = settle(parked_out, [second_grad, second_out] if LAST else [])
     return (
         second_out[None],
         second_grad[None],

time: 116 us -> 102 us (0.88)
  the two profiles are of different devices: /device:TPU:2 before, /device:TPU:1 now
where the time goes in v2:
time: 102 us; the launch traced here: 101 us
  starting transfers between devices  37.7 us (37%)
  Pallas kernels  32.3 us (32%)
  blocking collectives  11.3 us (11%)
  local copies, waits for them, and re-layouts  10.5 us (10%)
  waiting for transfers between devices  8.28 us (8%)
    pallas_call x6, Pallas kernels, call(): pl.pallas_call(body, name=name, out_shape=outs, in_specs=[SMEM if smem_fi...  27.7 us
    all_to_all x1, blocking collectives, gathered(): return lax.all_to_all(sums, 'tensor', 0, 0)  11.3 us
    all_to_all x2, starting transfers between devices, gathered(): return lax.all_to_all(sums, 'tensor', 0, 0)  10.8 us
    unnamed x34, local copies, waits for them, and re-layouts  10.5 us
    ppermute x1, starting transfers between devices, per_device(): parked_out = [lax.ppermute(parking_out, 'section', parking)]  10.5 us
    ppermute x1, starting transfers between devices, per_device(): fetched = [lax.ppermute(parked, 'section', mirrored)]  8.58 us
    ppermute x1, starting transfers between devices, per_device(): lax.ppermute(jnp.broadcast_to(stored_squares, (8, TOK)), 'section', mirro...  6.84 us
    ppermute x1, waiting for transfers between devices, per_device(): parked_out = [lax.ppermute(parking_out, 'section', parking)]  6.13 us
  transfers between devices with their start and end apart: 7, of which 2 were waited for; matrix products, arithmetic and copies ran while one was open for 0% of the time, Pallas kernels for 27%

profile of v2, /device:TPU:1, one launch (start us, length us, event | category | flops | bytes accessed | tf_op | source)
XLA Modules:
  0.0 100.9 jit_solution(7179338944461315074)
XLA Ops:
  0.6 0.0 copy-start
  0.6 0.0 copy-start.12
  0.7 0.0 copy-start.15
  0.7 0.0 copy-start.14
  0.7 0.0 copy-start.6
  0.7 2.6 %squares.1 = f32[8,8,256]{2,1,0:T(8,128)} custom-call(bf16[256,1536]{1,0:T(8,128)(2,1)} %bitcast.12, bf16[256,1536]{1,0:T(8,128)(2,1)} %bitcast.7, bf16[256,1536]{1,0:T(8,128)(2,1)} %bitcast.15), custom_call_target="tpu_custom_call" | custom-call | tf_op jit(solution)/shard_map/squares/pallas_call | solution.py:270
  3.3 6.0 %all-to-all-start = ((f32[8,8,256]{2,1,0:T(8,128)}), f32[8,8,256]{2,1,0:T(8,128)S(1)}, u32[]{:S(2)}, u32[]{:S(2)}) async-start(f32[8,8,256]{2,1,0:T(8,128)} %squares.1), calls=%async_computation | async-start | bytes 131072 | tf_op jit(solution)/shard_map/all_to_all | solution.py:356
  9.3 8.6 %collective-permute-start.1 = (bf16[256,1536]{1,0:T(8,128)(2,1)}, bf16[256,1536]{1,0:T(8,128)(2,1)S(1)}, u32[]{:S(2)}, u32[]{:S(2)}) collective-permute-start(bf16[256,1536]{1,0:T(8,128)(2,1)} %bitcast.16), channel_id=1, source_target_pairs={{0,248},{8,240},{16,232},{24,224},{32,216},{40,208},{48,200},{56,1... | collective-permute-start | bytes 2359304 | tf_op jit(solution)/shard_map/ppermute | solution.py:366
  17.8 0.0 all-to-all-done.refs_2_.refs_3_.refs_4_
  17.8 0.0 copy-done
  17.8 0.0 copy-done.12
  17.9 0.0 copy-done.15
  17.9 0.0 copy-done.14
  17.9 0.0 copy-done.6
  17.9 5.8 %backward_first.1 = (f32[256,1536]{1,0:T(8,128)S(1)}, f32[8,8,256]{2,1,0:T(8,128)}, f32[1,1536]{1,0:T(1,128)S(1)}, f32[1,1536]{1,0:T(1,128)S(1)}) custom-call(s32[65]{0:T(128)S(1)} %copy-done.12, bf16[256,1536]{1,0:T(8,128)(2,1)S(1)} %bitcast.8, bf16[256,1536]{1,0:T(8,128)(2,1)S(1)} %bitcast.10, f32[8,8,256]{2,1,0:T(8,128)S(1)} %all-to-all-done.refs_2_.refs_3_.refs_4_, ...), custom_call_target="tpu_custom_call" | custom-call | flops 6000000000 | bytes 3301636 | tf_op jit(solution)/shard_map/backward_first/pallas_call | solution.py:245
  23.7 0.0 copy-start.4
  23.7 1.2 %copy-done.4 = f32[256,1536]{1,0:T(8,128)} copy-done((f32[256,1536]{1,0:T(8,128)}, f32[256,1536]{1,0:T(8,128)S(1)}, u32[]{:S(2)}) %copy-start.4) | copy-done | bytes 1572888
  24.8 4.8 %all-to-all-start.1 = ((f32[8,8,256]{2,1,0:T(8,128)}), f32[8,8,256]{2,1,0:T(8,128)S(1)}, u32[]{:S(2)}, u32[]{:S(2)}) async-start(f32[8,8,256]{2,1,0:T(8,128)} %get-tuple-element.17), calls=%async_computation.1 | async-start | bytes 131072 | tf_op jit(solution)/shard_map/all_to_all | solution.py:356
  29.7 0.0 copy-start.8
  29.7 1.1 %copy-done.8 = bf16[1,256,1536]{2,1,0:T(8,128)(2,1)S(1)} copy-done((bf16[1,256,1536]{2,1,0:T(8,128)(2,1)S(1)}, bf16[1,256,1536]{2,1,0:T(8,128)(2,1)}, u32[]{:S(2)}) %copy-start.8) | copy-done | bytes 786456
  30.8 0.0 copy-start.13
  30.8 1.1 %copy-done.13 = bf16[256,1536]{1,0:T(8,128)(2,1)S(1)} copy-done((bf16[256,1536]{1,0:T(8,128)(2,1)S(1)}, bf16[256,1536]{1,0:T(8,128)(2,1)}, u32[]{:S(2)}) %copy-start.13) | copy-done | bytes 786456
  31.9 5.6 %forward_first.1 = (bf16[256,1536]{1,0:T(8,128)(2,1)}, bf16[256,1536]{1,0:T(8,128)(2,1)S(1)}) custom-call(s32[65]{0:T(128)S(1)} %copy-done.12, bf16[256,1536]{1,0:T(8,128)(2,1)S(1)} %bitcast.13, f32[8,8,256]{2,1,0:T(8,128)S(1)} %all-to-all-done.refs_2_.refs_3_.refs_4_, f32[1,1536]{1,0:T(1,128)S(1)} %copy-done.14, f32[1,1536]{1,0:T(1,128)S(1)} %copy-done.15, ...), custom_call_target="tpu_custom_call" | custom-call | flops 3000000000 | bytes 3223812 | tf_op jit(solution)/shard_map/forward_first/pallas_call | solution.py:245
  37.5 0.0 copy-start.9
  37.5 0.9 copy-done.9
  38.4 1.1 %collective-permute-start = (bf16[256,1536]{1,0:T(8,128)(2,1)}, bf16[256,1536]{1,0:T(8,128)(2,1)}, u32[]{:S(2)}, u32[]{:S(2)}) collective-permute-start(bf16[256,1536]{1,0:T(8,128)(2,1)} %get-tuple-element.15), channel_id=1, source_target_pairs={{0,8},{8,16},{16,24},{24,32},{32,40},{40,48},{48,56},{56,64},{64,7... | collective-permute-start | bytes 2359304 | tf_op jit(solution)/shard_map/ppermute | solution.py:393
  39.4 0.0 all-to-all-done.1.refs_5_
  39.4 0.0 copy-start.5
  39.4 1.4 %copy-done.5 = f32[256,1536]{1,0:T(8,128)S(1)} copy-done((f32[256,1536]{1,0:T(8,128)S(1)}, f32[256,1536]{1,0:T(8,128)}, u32[]{:S(2)}) %copy-start.5) | copy-done | bytes 1572888
  40.8 0.0 copy-start.7
  40.8 1.1 %copy-done.7 = bf16[256,1536]{1,0:T(8,128)(2,1)S(1)} copy-done((bf16[256,1536]{1,0:T(8,128)(2,1)S(1)}, bf16[256,1536]{1,0:T(8,128)(2,1)}, u32[]{:S(2)}) %copy-start.7) | copy-done | bytes 786456
  42.0 2.0 %finish_first.1 = bf16[256,1536]{1,0:T(8,128)(2,1)} custom-call(s32[65]{0:T(128)S(1)} %copy-done.12, bf16[256,1536]{1,0:T(8,128)(2,1)S(1)} %bitcast.9, bf16[256,1536]{1,0:T(8,128)(2,1)S(1)} %bitcast.11, f32[256,1536]{1,0:T(8,128)S(1)} %copy-done.5, f32[8,8,256]{2,1,0:T(8,128)S(1)} %all-to-all-done.refs_2_.refs_3_.refs_4_, ...), custom_call_target="tpu_custom_call" | custom-call | flops 1000000000 | bytes 4849924 | tf_op jit(solution)/shard_map/finish_first/pallas_call | solution.py:245
  44.0 0.0 collective-permute-start.2
  44.0 6.8 %collective-permute-start.3 = (f32[8,256]{1,0:T(8,128)S(1)}, f32[8,256]{1,0:T(8,128)S(1)}, u32[]{:S(2)}, u32[]{:S(2)}) collective-permute-start(f32[8,256]{1,0:T(8,128)S(1)} %broadcast_in_dim.15), channel_id=1, source_target_pairs={{0,248},{8,240},{16,232},{24,224},{32,216},{40,208},{48,200},{56,1... | collective-permute-start | bytes 24584 | tf_op jit(solution)/shard_map/ppermute | solution.py:374
  50.9 2.1 %collective-permute-done.3.refs_3_.refs_4_.refs_2_ = f32[8,256]{1,0:T(8,128)S(1)} collective-permute-done((f32[8,256]{1,0:T(8,128)S(1)}, f32[8,256]{1,0:T(8,128)S(1)}, u32[]{:S(2)}, u32[]{:S(2)}) %collective-permute-start.3) | collective-permute-done | bytes 8224 | tf_op jit(solution)/shard_map/ppermute | solution.py:374
  53.0 0.0 copy-start.10
  53.0 0.0 collective-permute-done.1.refs_1_
  53.0 0.0 copy-start.1
  53.0 0.6 copy-done.10
  53.6 0.3 copy-done.1
  53.9 10.5 %collective-permute-start.4 = (bf16[256,1536]{1,0:T(8,128)(2,1)}, bf16[256,1536]{1,0:T(8,128)(2,1)S(1)}, u32[]{:S(2)}, u32[]{:S(2)}) collective-permute-start(bf16[256,1536]{1,0:T(8,128)(2,1)} %hold.1), channel_id=1, source_target_pairs={{0,240},{8,232},{16,224},{24,216},{32,208},{40,200},{48,192},{56,1... | collective-permute-start | bytes 2359304 | tf_op jit(solution)/shard_map/ppermute | solution.py:395
  64.4 0.0 collective-permute-done.refs_8_.refs_1_
  64.4 0.0 collective-permute-done.2.refs_2_
  64.4 0.0 copy-start.2
  64.4 1.1 %copy-done.2 = bf16[256,1536]{1,0:T(8,128)(2,1)S(1)} copy-done((bf16[256,1536]{1,0:T(8,128)(2,1)S(1)}, bf16[256,1536]{1,0:T(8,128)(2,1)}, u32[]{:S(2)}) %copy-start.2) | copy-done | bytes 786456
  65.5 0.0 copy-start.11
  65.5 0.7 copy-done.11
  66.2 0.0 copy-start.3
  66.2 6.3 %backward_second.1 = (f32[256,1536]{1,0:T(8,128)S(1)}, f32[8,8,256]{2,1,0:T(8,128)S(1)}, f32[1,1536]{1,0:T(1,128)}, f32[1,1536]{1,0:T(1,128)}) custom-call(s32[65]{0:T(128)S(1)} %copy-done.12, bf16[256,1536]{1,0:T(8,128)(2,1)S(1)} %copy-done.2, bf16[256,1536]{1,0:T(8,128)(2,1)S(1)} %collective-permute-done.2.refs_2_, f32[8,256]{1,0:T(8,128)S(1)} %copy-done.11, ...), custom_call_target="tpu_custom_call" | custom-call | flops 6000000000 | bytes 4043012 | tf_op jit(solution)/shard_map/backward_second/pallas_call | solution.py:245
  72.5 11.3 %all_to_all.15.refs_2_.refs_5_ = f32[8,8,256]{2,1,0:T(8,128)S(1)} all-to-all(f32[8,8,256]{2,1,0:T(8,128)S(1)} %get-tuple-element.20), channel_id=1, replica_groups=mesh['section'=32,'tensor'=8] {'tensor'}, dimensions={0} | all-to-all | bytes 131072 | tf_op jit(solution)/shard_map/all_to_all | solution.py:356
  83.8 0.0 copy-done.3
  83.8 1.9 %finish_second.1.refs_1_ = bf16[256,1536]{1,0:T(8,128)(2,1)} custom-call(s32[65]{0:T(128)S(1)} %copy-done.12, bf16[256,1536]{1,0:T(8,128)(2,1)S(1)} %copy-done.3, bf16[256,1536]{1,0:T(8,128)(2,1)S(1)} %collective-permute-done.2.refs_2_, f32[256,1536]{1,0:T(8,128)S(1)} %get-tuple-element.21.refs_3_, f32[8,256]{1,0:T(8,128)S(1)} %copy-done.11, ...), custom_call_target="tpu_custom_call" | custom-call | flops 1000000000 | bytes 4006148 | tf_op jit(solution)/shard_map/finish_second/pallas_call | solution.py:245
  85.7 6.1 %forward_second.1.refs_2_ = bf16[256,1536]{1,0:T(8,128)(2,1)} custom-call(s32[65]{0:T(128)S(1)} %copy-done.12, bf16[256,1536]{1,0:T(8,128)(2,1)} %collective-permute-done.refs_8_.refs_1_, f32[8,8,256]{2,1,0:T(8,128)S(1)} %all_to_all.15.refs_2_.refs_5_, f32[1,1536]{1,0:T(1,128)S(1)} %copy-done.14, f32[1,1536]{1,0:T(1,128)S(1)} %copy-done.15), custom_call_target="tpu_custom_call" | custom-call | flops 3000000000 | bytes 1650948 | tf_op jit(solution)/shard_map/forward_second/pallas_call | solution.py:245
  91.9 6.1 %collective-permute-done.4.refs_0_ = bf16[256,1536]{1,0:T(8,128)(2,1)S(1)} collective-permute-done((bf16[256,1536]{1,0:T(8,128)(2,1)}, bf16[256,1536]{1,0:T(8,128)(2,1)S(1)}, u32[]{:S(2)}, u32[]{:S(2)}) %collective-permute-start.4) | collective-permute-done | bytes 786464 | tf_op jit(solution)/shard_map/ppermute | solution.py:395
  98.0 0.0 copy-start.16
  98.0 0.9 copy-done.16
  98.9 2.0 %settle.1 = bf16[256,1536]{1,0:T(8,128)(2,1)} custom-call(bf16[256,1536]{1,0:T(8,128)(2,1)} %copy-done.16, bf16[256,1536]{1,0:T(8,128)(2,1)} %finish_second.1.refs_1_, bf16[256,1536]{1,0:T(8,128)(2,1)} %forward_second.1.refs_2_), custom_call_target="tpu_custom_call" | custom-call | tf_op jit(solution)/shard_map/settle/pallas_call | solution.py:330
  (3 shorter events, 0.0 us)
Async XLA Ops:
  0.6 17.2 %copy-start = (bf16[1,256,1536]{2,1,0:T(8,128)(2,1)S(1)}, bf16[1,256,1536]{2,1,0:T(8,128)(2,1)}, u32[]{:S(2)}) copy-start(bf16[1,256,1536]{2,1,0:T(8,128)(2,1)} %param.11) | copy-start | bytes 2359300
  0.6 17.2 %copy-start.12 = (s32[65]{0:T(128)S(1)}, s32[65]{0:T(128)}, u32[]{:S(2)}) copy-start(s32[65]{0:T(128)} %refs_0_.11) | copy-start | bytes 784
  0.7 17.2 %copy-start.15 = (f32[1,1536]{1,0:T(1,128)S(1)}, f32[1,1536]{1,0:T(1,128)}, u32[]{:S(2)}) copy-start(f32[1,1536]{1,0:T(1,128)} %refs_4_.7) | copy-start | bytes 18436
  0.7 17.2 %copy-start.14 = (f32[1,1536]{1,0:T(1,128)S(1)}, f32[1,1536]{1,0:T(1,128)}, u32[]{:S(2)}) copy-start(f32[1,1536]{1,0:T(1,128)} %refs_3_.3) | copy-start | bytes 18436
  0.7 17.2 %copy-start.6 = (bf16[1,256,1536]{2,1,0:T(8,128)(2,1)S(1)}, bf16[1,256,1536]{2,1,0:T(8,128)(2,1)}, u32[]{:S(2)}) copy-start(bf16[1,256,1536]{2,1,0:T(8,128)(2,1)} %param.10) | copy-start | bytes 2359300
  3.3 14.5 %all-to-all-start = ((f32[8,8,256]{2,1,0:T(8,128)}), f32[8,8,256]{2,1,0:T(8,128)S(1)}, u32[]{:S(2)}, u32[]{:S(2)}) async-start(f32[8,8,256]{2,1,0:T(8,128)} %squares.1), calls=%async_computation | async-start | bytes 131072 | tf_op jit(solution)/shard_map/all_to_all | solution.py:356
  9.3 43.7 %collective-permute-start.1 = (bf16[256,1536]{1,0:T(8,128)(2,1)}, bf16[256,1536]{1,0:T(8,128)(2,1)S(1)}, u32[]{:S(2)}, u32[]{:S(2)}) collective-permute-start(bf16[256,1536]{1,0:T(8,128)(2,1)} %bitcast.16), channel_id=1, source_target_pairs={{0,248},{8,240},{16,232},{24,224},{32,216},{40,208},{48,200},{56,1... | collective-permute-start | bytes 2359304 | tf_op jit(solution)/shard_map/ppermute | solution.py:366
  23.7 1.2 %copy-start.4 = (f32[256,1536]{1,0:T(8,128)}, f32[256,1536]{1,0:T(8,128)S(1)}, u32[]{:S(2)}) copy-start(f32[256,1536]{1,0:T(8,128)S(1)} %get-tuple-element.16.refs_3_) | copy-start | bytes 4718596
  24.8 14.6 %all-to-all-start.1 = ((f32[8,8,256]{2,1,0:T(8,128)}), f32[8,8,256]{2,1,0:T(8,128)S(1)}, u32[]{:S(2)}, u32[]{:S(2)}) async-start(f32[8,8,256]{2,1,0:T(8,128)} %get-tuple-element.17), calls=%async_computation.1 | async-start | bytes 131072 | tf_op jit(solution)/shard_map/all_to_all | solution.py:356
  29.7 1.1 %copy-start.8 = (bf16[1,256,1536]{2,1,0:T(8,128)(2,1)S(1)}, bf16[1,256,1536]{2,1,0:T(8,128)(2,1)}, u32[]{:S(2)}) copy-start(bf16[1,256,1536]{2,1,0:T(8,128)(2,1)} %param.9) | copy-start | bytes 2359300
  30.8 1.1 %copy-start.13 = (bf16[256,1536]{1,0:T(8,128)(2,1)S(1)}, bf16[256,1536]{1,0:T(8,128)(2,1)}, u32[]{:S(2)}) copy-start(bf16[256,1536]{1,0:T(8,128)(2,1)} %refs_5_.3) | copy-start | bytes 2359300
  37.5 0.9 copy-start.9
  38.4 26.0 %collective-permute-start = (bf16[256,1536]{1,0:T(8,128)(2,1)}, bf16[256,1536]{1,0:T(8,128)(2,1)}, u32[]{:S(2)}, u32[]{:S(2)}) collective-permute-start(bf16[256,1536]{1,0:T(8,128)(2,1)} %get-tuple-element.15), channel_id=1, source_target_pairs={{0,8},{8,16},{16,24},{24,32},{32,40},{40,48},{48,56},{56,64},{64,7... | collective-permute-start | bytes 2359304 | tf_op jit(solution)/shard_map/ppermute | solution.py:393
  39.4 1.4 %copy-start.5 = (f32[256,1536]{1,0:T(8,128)S(1)}, f32[256,1536]{1,0:T(8,128)}, u32[]{:S(2)}) copy-start(f32[256,1536]{1,0:T(8,128)} %copy-done.4) | copy-start | bytes 4718596
  40.8 1.1 %copy-start.7 = (bf16[256,1536]{1,0:T(8,128)(2,1)S(1)}, bf16[256,1536]{1,0:T(8,128)(2,1)}, u32[]{:S(2)}) copy-start(bf16[256,1536]{1,0:T(8,128)(2,1)} %refs_6_.1) | copy-start | bytes 2359300
  44.0 20.4 %collective-permute-start.2 = (bf16[256,1536]{1,0:T(8,128)(2,1)}, bf16[256,1536]{1,0:T(8,128)(2,1)S(1)}, u32[]{:S(2)}, u32[]{:S(2)}) collective-permute-start(bf16[256,1536]{1,0:T(8,128)(2,1)} %finish_first.1), channel_id=1, source_target_pairs={{8,0},{16,8},{24,16},{32,24},{40,32},{48,40},{56,48},{64,56},{72,6... | collective-permute-start | bytes 2359304 | tf_op jit(solution)/shard_map/ppermute | solution.py:385
  44.0 9.0 %collective-permute-start.3 = (f32[8,256]{1,0:T(8,128)S(1)}, f32[8,256]{1,0:T(8,128)S(1)}, u32[]{:S(2)}, u32[]{:S(2)}) collective-permute-start(f32[8,256]{1,0:T(8,128)S(1)} %broadcast_in_dim.15), channel_id=1, source_target_pairs={{0,248},{8,240},{16,232},{24,224},{32,216},{40,208},{48,200},{56,1... | collective-permute-start | bytes 24584 | tf_op jit(solution)/shard_map/ppermute | solution.py:374
  53.0 0.6 copy-start.10
  53.0 0.9 copy-start.1
  53.9 44.1 %collective-permute-start.4 = (bf16[256,1536]{1,0:T(8,128)(2,1)}, bf16[256,1536]{1,0:T(8,128)(2,1)S(1)}, u32[]{:S(2)}, u32[]{:S(2)}) collective-permute-start(bf16[256,1536]{1,0:T(8,128)(2,1)} %hold.1), channel_id=1, source_target_pairs={{0,240},{8,232},{16,224},{24,216},{32,208},{40,200},{48,192},{56,1... | collective-permute-start | bytes 2359304 | tf_op jit(solution)/shard_map/ppermute | solution.py:395
  64.4 1.1 %copy-start.2 = (bf16[256,1536]{1,0:T(8,128)(2,1)S(1)}, bf16[256,1536]{1,0:T(8,128)(2,1)}, u32[]{:S(2)}) copy-start(bf16[256,1536]{1,0:T(8,128)(2,1)} %copy-done.1) | copy-start | bytes 2359300
  65.5 0.7 copy-start.11
  66.2 17.5 %copy-start.3 = (bf16[256,1536]{1,0:T(8,128)(2,1)S(1)}, bf16[256,1536]{1,0:T(8,128)(2,1)}, u32[]{:S(2)}) copy-start(bf16[256,1536]{1,0:T(8,128)(2,1)} %copy-done.1) | copy-start | bytes 2359300
  98.0 0.9 copy-start.16

commit v3 on v2

--- a/solution.py
+++ b/solution.py
@@ -14,12 +14,13 @@
 EPSILON = 1e-05
 LOG2E = 1.4426950408889634
 MASKED = -1e30
-VMEM_LIMIT = 40 * 1024 * 1024
+VMEM_LIMIT = 20 * 1024 * 1024
+SMALL_VMEM = 2 * 1024 * 1024
 WHOLE_VMEM = 62 * 1024 * 1024
 UNROLL = 6
 COST = 1.0
-AFTER = ((), (), (), ('m', 'tm', ), (), (), ())
-LAST = True
+AFTER = ((), (), (), ("m0", "tm"), (), (), ())
+MIRROR_ROWS = (256,)
 HOLD = True
 
 ROWS_ROWS = (((1,), (1,)), ((), ()))
@@ -116,7 +117,8 @@
     if select:
         other_ref, y_ref, copy_ref, inv, bias = rest
     else:
-        y_ref, inv, bias = rest
+        y_ref, mark_ref, inv, bias = rest
+        mark_ref[...] = jnp.zeros_like(mark_ref)
     if pick is None:
         row = sums_ref[0:1, :]
     else:
@@ -289,8 +291,8 @@
 def forward_second(micro, lens, x, sums, gain, qgain, after=()):
     return call(
         functools.partial(forward_kernel, micro, 1, False), "forward_second",
-        [lens, x, sums, gain, qgain], [shape(x.shape, jnp.bfloat16)], [COLS, BIAS], 3 * 10**9, True, after,
-    )[0]
+        [lens, x, sums, gain, qgain], [shape(x.shape, jnp.bfloat16), shape((8, HD), jnp.float32)], [COLS, BIAS], 3 * 10**9, True, after,
+    )
 
 
 def backward_call(micro, first, lens, x, dy, sums, gain, qgain, rest, after=()):
@@ -334,6 +336,7 @@
         in_specs=[VMEM] * len(parts) + [pl.BlockSpec(memory_space=pl.ANY)] * len(after),
         out_specs=pl.BlockSpec(memory_space=pltpu.HBM),
         scratch_shapes=[pltpu.SemaphoreType.DMA((len(parts),))],
+        compiler_params=pltpu.CompilerParams(vmem_limit_bytes=SMALL_VMEM),
     )(*parts, *after)
 
 
@@ -349,6 +352,7 @@
         in_specs=[pl.BlockSpec(memory_space=pl.ANY)] * (1 + len(after)),
         out_specs=pl.BlockSpec(memory_space=pl.ANY),
         input_output_aliases={0: 0},
+        compiler_params=pltpu.CompilerParams(vmem_limit_bytes=SMALL_VMEM),
     )(value, *after)
 
 
@@ -363,8 +367,12 @@
     onward = [(i, (i + 1) % count) for i in range(count)]
     back = [((i + 1) % count, i) for i in range(count)]
     x, dy, stored, parked = x_in[0], grad_in[0], stash_near[0], parked_in[0]
-    fetched = [lax.ppermute(parked, "section", mirrored)]
-    made = {"m": fetched[0]}
+    fetched = []
+    at = 0
+    for rows_n in MIRROR_ROWS:
+        fetched.append(lax.ppermute(parked[at : at + rows_n], "section", mirrored))
+        at += rows_n
+    made = {f"m{i}": part for i, part in enumerate(fetched)}
 
     def after(k):
         return [made[n] for n in AFTER[k]]
@@ -401,10 +409,10 @@
     second_grad = finish_call(
         False, lengths, fetched, d_two, d_unit, stored_squares, project, [], after(5)
     )[0]
-    second_out = forward_second(
+    second_out, mark = forward_second(
         lambda s: 2 * count - s, lengths, x_two, project, gain, qgain, after(6)
     )
-    parked_out = settle(parked_out, [second_grad, second_out] if LAST else [])
+    parked_out = settle(parked_out, [mark])
     return (
         second_out[None],
         second_grad[None],

time: 102 us -> 97.4 us (0.955)
  local copies, waits for them, and re-layouts: 10.5 us -> 6.88 us
  waiting for transfers between devices: 8.28 us -> 11.2 us
  Pallas kernels: 32.3 us -> 30.2 us
    unnamed x34 -> x24, local copies, waits for them, and re-layouts: 10.5 us -> 6.87 us
    ppermute x1, waiting for transfers between devices: 6.13 us -> 8.16 us  [per_device(): parked_out = [lax.ppermute(parking_out, 'section', parking)]]
    pallas_call x1, Pallas kernels: 2.02 us -> 0.89 us  [settle(): pl.pallas_call(functools.partial(settle_kernel, len(parts)), name='settle...]
    ppermute x1, starting transfers between devices: 10.5 us -> 9.39 us  [per_device(): parked_out = [lax.ppermute(parking_out, 'section', parking)]]
  transfers between devices with their start and end apart: 7 -> 7, of which waited for: 2 -> 2; matrix products, arithmetic and copies ran while one was open for 0% -> 0% of each run, Pallas kernels for 27% -> 28%
where the time goes in v3:
time: 97.4 us; the launch traced here: 96.8 us
  starting transfers between devices  36.8 us (38%)
  Pallas kernels  30.2 us (31%)
  waiting for transfers between devices  11.2 us (11%)
  blocking collectives  11 us (11%)
  local copies, waits for them, and re-layouts  6.88 us (7%)
    pallas_call x6, Pallas kernels, call(): pl.pallas_call(body, name=name, out_shape=outs, in_specs=[SMEM if smem_fi...  26.8 us
    all_to_all x1, blocking collectives, gathered(): return lax.all_to_all(sums, 'tensor', 0, 0)  11 us
    all_to_all x2, starting transfers between devices, gathered(): return lax.all_to_all(sums, 'tensor', 0, 0)  10.8 us
    ppermute x1, starting transfers between devices, per_device(): parked_out = [lax.ppermute(parking_out, 'section', parking)]  9.39 us
    ppermute x1, starting transfers between devices, per_device(): fetched.append(lax.ppermute(parked[at:at + rows_n], 'section', mirrored))  8.58 us
    ppermute x1, waiting for transfers between devices, per_device(): parked_out = [lax.ppermute(parking_out, 'section', parking)]  8.16 us
    unnamed x24, local copies, waits for them, and re-layouts  6.87 us
    ppermute x1, starting transfers between devices, per_device(): lax.ppermute(jnp.broadcast_to(stored_squares, (8, TOK)), 'section', mirro...  6.85 us
  transfers between devices with their start and end apart: 7, of which 2 were waited for; matrix products, arithmetic and copies ran while one was open for 0% of the time, Pallas kernels for 28%

profile of v3, /device:TPU:1, one launch (start us, length us, event | category | flops | bytes accessed | tf_op | source)
XLA Modules:
  0.0 96.8 jit_solution(11759352639569690408)
XLA Ops:
  0.6 0.0 copy-start
  0.6 0.0 copy-start.8
  0.7 0.0 copy-start.11
  0.7 0.0 copy-start.10
  0.7 0.0 copy-start.3
  0.7 2.6 %squares.1 = f32[8,8,256]{2,1,0:T(8,128)} custom-call(bf16[256,1536]{1,0:T(8,128)(2,1)} %bitcast.12, bf16[256,1536]{1,0:T(8,128)(2,1)} %bitcast.7, bf16[256,1536]{1,0:T(8,128)(2,1)} %bitcast.15), custom_call_target="tpu_custom_call" | custom-call | tf_op jit(solution)/shard_map/squares/pallas_call | solution.py:272
  3.3 6.0 %all-to-all-start = ((f32[8,8,256]{2,1,0:T(8,128)}), f32[8,8,256]{2,1,0:T(8,128)S(1)}, u32[]{:S(2)}, u32[]{:S(2)}) async-start(f32[8,8,256]{2,1,0:T(8,128)} %squares.1), calls=%async_computation | async-start | bytes 131072 | tf_op jit(solution)/shard_map/all_to_all | solution.py:360
  9.3 8.6 %collective-permute-start.1 = (bf16[256,1536]{1,0:T(8,128)(2,1)}, bf16[256,1536]{1,0:T(8,128)(2,1)S(1)}, u32[]{:S(2)}, u32[]{:S(2)}) collective-permute-start(bf16[256,1536]{1,0:T(8,128)(2,1)} %bitcast.16), channel_id=1, source_target_pairs={{0,248},{8,240},{16,232},{24,224},{32,216},{40,208},{48,200},{56,1... | collective-permute-start | bytes 2359304 | tf_op jit(solution)/shard_map/ppermute | solution.py:373
  17.8 0.0 all-to-all-done.refs_2_.refs_3_.refs_4_
  17.8 0.0 copy-done
  17.8 0.0 copy-done.8
  17.9 0.0 copy-done.11
  17.9 0.0 copy-done.10
  17.9 0.0 copy-done.3
  17.9 5.8 %backward_first.1 = (f32[256,1536]{1,0:T(8,128)S(1)}, f32[8,8,256]{2,1,0:T(8,128)}, f32[1,1536]{1,0:T(1,128)S(1)}, f32[1,1536]{1,0:T(1,128)S(1)}) custom-call(s32[65]{0:T(128)S(1)} %copy-done.8, bf16[256,1536]{1,0:T(8,128)(2,1)S(1)} %bitcast.8, bf16[256,1536]{1,0:T(8,128)(2,1)S(1)} %bitcast.10, f32[8,8,256]{2,1,0:T(8,128)S(1)} %all-to-all-done.refs_2_.refs_3_.refs_4_, ...), custom_call_target="tpu_custom_call" | custom-call | flops 6000000000 | bytes 3301636 | tf_op jit(solution)/shard_map/backward_first/pallas_call | solution.py:247
  23.7 0.0 copy-start.1
  23.7 1.2 %copy-done.1 = f32[256,1536]{1,0:T(8,128)} copy-done((f32[256,1536]{1,0:T(8,128)}, f32[256,1536]{1,0:T(8,128)S(1)}, u32[]{:S(2)}) %copy-start.1) | copy-done | bytes 1572888
  24.8 4.8 %all-to-all-start.1 = ((f32[8,8,256]{2,1,0:T(8,128)}), f32[8,8,256]{2,1,0:T(8,128)S(1)}, u32[]{:S(2)}, u32[]{:S(2)}) async-start(f32[8,8,256]{2,1,0:T(8,128)} %get-tuple-element.19), calls=%async_computation.1 | async-start | bytes 131072 | tf_op jit(solution)/shard_map/all_to_all | solution.py:360
  29.6 0.0 copy-start.5
  29.6 1.1 %copy-done.5 = bf16[1,256,1536]{2,1,0:T(8,128)(2,1)S(1)} copy-done((bf16[1,256,1536]{2,1,0:T(8,128)(2,1)S(1)}, bf16[1,256,1536]{2,1,0:T(8,128)(2,1)}, u32[]{:S(2)}) %copy-start.5) | copy-done | bytes 786456
  30.8 0.0 copy-start.9
  30.8 1.1 %copy-done.9 = bf16[256,1536]{1,0:T(8,128)(2,1)S(1)} copy-done((bf16[256,1536]{1,0:T(8,128)(2,1)S(1)}, bf16[256,1536]{1,0:T(8,128)(2,1)}, u32[]{:S(2)}) %copy-start.9) | copy-done | bytes 786456
  31.9 5.5 %forward_first.1 = (bf16[256,1536]{1,0:T(8,128)(2,1)}, bf16[256,1536]{1,0:T(8,128)(2,1)S(1)}) custom-call(s32[65]{0:T(128)S(1)} %copy-done.8, bf16[256,1536]{1,0:T(8,128)(2,1)S(1)} %bitcast.13, f32[8,8,256]{2,1,0:T(8,128)S(1)} %all-to-all-done.refs_2_.refs_3_.refs_4_, f32[1,1536]{1,0:T(1,128)S(1)} %copy-done.10, f32[1,1536]{1,0:T(1,128)S(1)} %copy-done.11, ...), custom_call_target="tpu_custom_call" | custom-call | flops 3000000000 | bytes 3223812 | tf_op jit(solution)/shard_map/forward_first/pallas_call | solution.py:247
  37.5 0.0 copy-start.6
  37.5 0.9 copy-done.6
  38.3 1.1 %collective-permute-start = (bf16[256,1536]{1,0:T(8,128)(2,1)}, bf16[256,1536]{1,0:T(8,128)(2,1)}, u32[]{:S(2)}, u32[]{:S(2)}) collective-permute-start(bf16[256,1536]{1,0:T(8,128)(2,1)} %get-tuple-element.17), channel_id=1, source_target_pairs={{0,8},{8,16},{16,24},{24,32},{32,40},{40,48},{48,56},{56,64},{64,7... | collective-permute-start | bytes 2359304 | tf_op jit(solution)/shard_map/ppermute | solution.py:401
  39.4 0.0 all-to-all-done.1.refs_5_
  39.4 0.0 copy-start.2
  39.4 1.4 %copy-done.2 = f32[256,1536]{1,0:T(8,128)S(1)} copy-done((f32[256,1536]{1,0:T(8,128)S(1)}, f32[256,1536]{1,0:T(8,128)}, u32[]{:S(2)}) %copy-start.2) | copy-done | bytes 1572888
  40.8 0.0 copy-start.4
  40.8 1.1 %copy-done.4 = bf16[256,1536]{1,0:T(8,128)(2,1)S(1)} copy-done((bf16[256,1536]{1,0:T(8,128)(2,1)S(1)}, bf16[256,1536]{1,0:T(8,128)(2,1)}, u32[]{:S(2)}) %copy-start.4) | copy-done | bytes 786456
  42.0 0.0 copy-start.7
  42.0 1.1 %finish_first.1 = bf16[256,1536]{1,0:T(8,128)(2,1)S(1)} custom-call(s32[65]{0:T(128)S(1)} %copy-done.8, bf16[256,1536]{1,0:T(8,128)(2,1)S(1)} %bitcast.9, bf16[256,1536]{1,0:T(8,128)(2,1)S(1)} %bitcast.11, f32[256,1536]{1,0:T(8,128)S(1)} %copy-done.2, f32[8,8,256]{2,1,0:T(8,128)S(1)} %all-to-all-done.refs_2_.refs_3_.refs_4_, ...), custom_call_target="tpu_custom_call" | custom-call | flops 1000000000 | bytes 4849924 | tf_op jit(solution)/shard_map/finish_first/pallas_call | solution.py:247
  43.1 0.1 collective-permute-start.2
  43.2 6.9 %collective-permute-start.3 = (f32[8,256]{1,0:T(8,128)S(1)}, f32[8,256]{1,0:T(8,128)S(1)}, u32[]{:S(2)}, u32[]{:S(2)}) collective-permute-start(f32[8,256]{1,0:T(8,128)S(1)} %broadcast_in_dim.15), channel_id=1, source_target_pairs={{0,248},{8,240},{16,232},{24,224},{32,216},{40,208},{48,200},{56,1... | collective-permute-start | bytes 24584 | tf_op jit(solution)/shard_map/ppermute | solution.py:382
  50.1 3.0 %collective-permute-done.3.refs_3_.refs_4_.refs_2_ = f32[8,256]{1,0:T(8,128)S(1)} collective-permute-done((f32[8,256]{1,0:T(8,128)S(1)}, f32[8,256]{1,0:T(8,128)S(1)}, u32[]{:S(2)}, u32[]{:S(2)}) %collective-permute-start.3) | collective-permute-done | bytes 8224 | tf_op jit(solution)/shard_map/ppermute | solution.py:382
  53.1 0.0 collective-permute-done.1.refs_1_
  53.1 0.0 copy-done.7
  53.1 9.4 %collective-permute-start.4 = (bf16[256,1536]{1,0:T(8,128)(2,1)S(1)}, bf16[256,1536]{1,0:T(8,128)(2,1)S(1)}, u32[]{:S(2)}, u32[]{:S(2)}) collective-permute-start(bf16[256,1536]{1,0:T(8,128)(2,1)S(1)} %hold.1), channel_id=1, source_target_pairs={{0,240},{8,232},{16,224},{24,216},{32,208},{40,200},{48,192},{56,1... | collective-permute-start | bytes 2359304 | tf_op jit(solution)/shard_map/ppermute | solution.py:403
  62.5 0.0 collective-permute-done.refs_8_.refs_1_
  62.5 0.0 collective-permute-done.2.refs_2_
  62.5 6.2 %backward_second.1 = (f32[256,1536]{1,0:T(8,128)S(1)}, f32[8,8,256]{2,1,0:T(8,128)S(1)}, f32[1,1536]{1,0:T(1,128)}, f32[1,1536]{1,0:T(1,128)}) custom-call(s32[65]{0:T(128)S(1)} %copy-done.8, bf16[256,1536]{1,0:T(8,128)(2,1)S(1)} %collective-permute-done.1.refs_1_, bf16[256,1536]{1,0:T(8,128)(2,1)S(1)} %collective-permute-done.2.refs_2_, ...), custom_call_target="tpu_custom_call" | custom-call | flops 6000000000 | bytes 4043012 | tf_op jit(solution)/shard_map/backward_second/pallas_call | solution.py:247
  68.7 11.0 %all_to_all.15.refs_2_.refs_5_ = f32[8,8,256]{2,1,0:T(8,128)S(1)} all-to-all(f32[8,8,256]{2,1,0:T(8,128)S(1)} %get-tuple-element.22), channel_id=1, replica_groups=mesh['section'=32,'tensor'=8] {'tensor'}, dimensions={0} | all-to-all | bytes 131072 | tf_op jit(solution)/shard_map/all_to_all | solution.py:360
  79.7 1.9 %finish_second.1 = bf16[256,1536]{1,0:T(8,128)(2,1)} custom-call(s32[65]{0:T(128)S(1)} %copy-done.8, bf16[256,1536]{1,0:T(8,128)(2,1)S(1)} %collective-permute-done.1.refs_1_, bf16[256,1536]{1,0:T(8,128)(2,1)S(1)} %collective-permute-done.2.refs_2_, f32[256,1536]{1,0:T(8,128)S(1)} %get-tuple-element.24.refs_3_, ...), custom_call_target="tpu_custom_call" | custom-call | flops 1000000000 | bytes 4006148 | tf_op jit(solution)/shard_map/finish_second/pallas_call | solution.py:247
  81.6 6.1 %forward_second.1 = (bf16[256,1536]{1,0:T(8,128)(2,1)}, f32[8,128]{1,0:T(8,128)S(1)}) custom-call(s32[65]{0:T(128)S(1)} %copy-done.8, bf16[256,1536]{1,0:T(8,128)(2,1)} %collective-permute-done.refs_8_.refs_1_, f32[8,8,256]{2,1,0:T(8,128)S(1)} %all_to_all.15.refs_2_.refs_5_, f32[1,1536]{1,0:T(1,128)S(1)} %copy-done.10, f32[1,1536]{1,0:T(1,128)S(1)} %copy-done.11), custom_call_target="tpu_custom_call" | custom-call | flops 3000000000 | bytes 1655044 | tf_op jit(solution)/shard_map/forward_second/pallas_call | solution.py:247
  87.8 8.2 %collective-permute-done.4.refs_0_ = bf16[256,1536]{1,0:T(8,128)(2,1)S(1)} collective-permute-done((bf16[256,1536]{1,0:T(8,128)(2,1)S(1)}, bf16[256,1536]{1,0:T(8,128)(2,1)S(1)}, u32[]{:S(2)}, u32[]{:S(2)}) %collective-permute-start.4) | collective-permute-done | bytes 786464 | tf_op jit(solution)/shard_map/ppermute | solution.py:403
  95.9 0.9 settle.1
  (3 shorter events, 0.0 us)
Async XLA Ops:
  0.6 17.2 %copy-start = (bf16[1,256,1536]{2,1,0:T(8,128)(2,1)S(1)}, bf16[1,256,1536]{2,1,0:T(8,128)(2,1)}, u32[]{:S(2)}) copy-start(bf16[1,256,1536]{2,1,0:T(8,128)(2,1)} %param.11) | copy-start | bytes 2359300
  0.6 17.2 %copy-start.8 = (s32[65]{0:T(128)S(1)}, s32[65]{0:T(128)}, u32[]{:S(2)}) copy-start(s32[65]{0:T(128)} %refs_0_.11) | copy-start | bytes 784
  0.7 17.2 %copy-start.11 = (f32[1,1536]{1,0:T(1,128)S(1)}, f32[1,1536]{1,0:T(1,128)}, u32[]{:S(2)}) copy-start(f32[1,1536]{1,0:T(1,128)} %refs_4_.7) | copy-start | bytes 18436
  0.7 17.2 %copy-start.10 = (f32[1,1536]{1,0:T(1,128)S(1)}, f32[1,1536]{1,0:T(1,128)}, u32[]{:S(2)}) copy-start(f32[1,1536]{1,0:T(1,128)} %refs_3_.3) | copy-start | bytes 18436
  0.7 17.2 %copy-start.3 = (bf16[1,256,1536]{2,1,0:T(8,128)(2,1)S(1)}, bf16[1,256,1536]{2,1,0:T(8,128)(2,1)}, u32[]{:S(2)}) copy-start(bf16[1,256,1536]{2,1,0:T(8,128)(2,1)} %param.10) | copy-start | bytes 2359300
  3.3 14.5 %all-to-all-start = ((f32[8,8,256]{2,1,0:T(8,128)}), f32[8,8,256]{2,1,0:T(8,128)S(1)}, u32[]{:S(2)}, u32[]{:S(2)}) async-start(f32[8,8,256]{2,1,0:T(8,128)} %squares.1), calls=%async_computation | async-start | bytes 131072 | tf_op jit(solution)/shard_map/all_to_all | solution.py:360
  9.3 43.8 %collective-permute-start.1 = (bf16[256,1536]{1,0:T(8,128)(2,1)}, bf16[256,1536]{1,0:T(8,128)(2,1)S(1)}, u32[]{:S(2)}, u32[]{:S(2)}) collective-permute-start(bf16[256,1536]{1,0:T(8,128)(2,1)} %bitcast.16), channel_id=1, source_target_pairs={{0,248},{8,240},{16,232},{24,224},{32,216},{40,208},{48,200},{56,1... | collective-permute-start | bytes 2359304 | tf_op jit(solution)/shard_map/ppermute | solution.py:373
  23.7 1.2 %copy-start.1 = (f32[256,1536]{1,0:T(8,128)}, f32[256,1536]{1,0:T(8,128)S(1)}, u32[]{:S(2)}) copy-start(f32[256,1536]{1,0:T(8,128)S(1)} %get-tuple-element.18.refs_3_) | copy-start | bytes 4718596
  24.8 14.6 %all-to-all-start.1 = ((f32[8,8,256]{2,1,0:T(8,128)}), f32[8,8,256]{2,1,0:T(8,128)S(1)}, u32[]{:S(2)}, u32[]{:S(2)}) async-start(f32[8,8,256]{2,1,0:T(8,128)} %get-tuple-element.19), calls=%async_computation.1 | async-start | bytes 131072 | tf_op jit(solution)/shard_map/all_to_all | solution.py:360
  29.6 1.1 %copy-start.5 = (bf16[1,256,1536]{2,1,0:T(8,128)(2,1)S(1)}, bf16[1,256,1536]{2,1,0:T(8,128)(2,1)}, u32[]{:S(2)}) copy-start(bf16[1,256,1536]{2,1,0:T(8,128)(2,1)} %param.9) | copy-start | bytes 2359300
  30.8 1.1 %copy-start.9 = (bf16[256,1536]{1,0:T(8,128)(2,1)S(1)}, bf16[256,1536]{1,0:T(8,128)(2,1)}, u32[]{:S(2)}) copy-start(bf16[256,1536]{1,0:T(8,128)(2,1)} %refs_5_.3) | copy-start | bytes 2359300
  37.5 0.9 copy-start.6
  38.3 24.2 %collective-permute-start = (bf16[256,1536]{1,0:T(8,128)(2,1)}, bf16[256,1536]{1,0:T(8,128)(2,1)}, u32[]{:S(2)}, u32[]{:S(2)}) collective-permute-start(bf16[256,1536]{1,0:T(8,128)(2,1)} %get-tuple-element.17), channel_id=1, source_target_pairs={{0,8},{8,16},{16,24},{24,32},{32,40},{40,48},{48,56},{56,64},{64,7... | collective-permute-start | bytes 2359304 | tf_op jit(solution)/shard_map/ppermute | solution.py:401
  39.4 1.4 %copy-start.2 = (f32[256,1536]{1,0:T(8,128)S(1)}, f32[256,1536]{1,0:T(8,128)}, u32[]{:S(2)}) copy-start(f32[256,1536]{1,0:T(8,128)} %copy-done.1) | copy-start | bytes 4718596
  40.8 1.1 %copy-start.4 = (bf16[256,1536]{1,0:T(8,128)(2,1)S(1)}, bf16[256,1536]{1,0:T(8,128)(2,1)}, u32[]{:S(2)}) copy-start(bf16[256,1536]{1,0:T(8,128)(2,1)} %refs_6_.1) | copy-start | bytes 2359300
  42.0 11.1 %copy-start.7 = (bf16[256,1536]{1,0:T(8,128)(2,1)S(1)}, bf16[256,1536]{1,0:T(8,128)(2,1)}, u32[]{:S(2)}) copy-start(bf16[256,1536]{1,0:T(8,128)(2,1)} %copy-done.6) | copy-start | bytes 2359300
  43.1 19.4 %collective-permute-start.2 = (bf16[256,1536]{1,0:T(8,128)(2,1)S(1)}, bf16[256,1536]{1,0:T(8,128)(2,1)S(1)}, u32[]{:S(2)}, u32[]{:S(2)}) collective-permute-start(bf16[256,1536]{1,0:T(8,128)(2,1)S(1)} %finish_first.1), channel_id=1, source_target_pairs={{8,0},{16,8},{24,16},{32,24},{40,32},{48,40},{56,48},{64,56},{72,6... | collective-permute-start | bytes 2359304 | tf_op jit(solution)/shard_map/ppermute | solution.py:393
  43.2 9.9 %collective-permute-start.3 = (f32[8,256]{1,0:T(8,128)S(1)}, f32[8,256]{1,0:T(8,128)S(1)}, u32[]{:S(2)}, u32[]{:S(2)}) collective-permute-start(f32[8,256]{1,0:T(8,128)S(1)} %broadcast_in_dim.15), channel_id=1, source_target_pairs={{0,248},{8,240},{16,232},{24,224},{32,216},{40,208},{48,200},{56,1... | collective-permute-start | bytes 24584 | tf_op jit(solution)/shard_map/ppermute | solution.py:382
  53.1 42.8 %collective-permute-start.4 = (bf16[256,1536]{1,0:T(8,128)(2,1)S(1)}, bf16[256,1536]{1,0:T(8,128)(2,1)S(1)}, u32[]{:S(2)}, u32[]{:S(2)}) collective-permute-start(bf16[256,1536]{1,0:T(8,128)(2,1)S(1)} %hold.1), channel_id=1, source_target_pairs={{0,240},{8,232},{16,224},{24,216},{32,208},{40,200},{48,192},{56,1... | collective-permute-start | bytes 2359304 | tf_op jit(solution)/shard_map/ppermute | solution.py:403

commit v4 on v3

--- a/solution.py
+++ b/solution.py
@@ -17,7 +17,7 @@
 VMEM_LIMIT = 20 * 1024 * 1024
 SMALL_VMEM = 2 * 1024 * 1024
 WHOLE_VMEM = 62 * 1024 * 1024
-UNROLL = 6
+UNROLL = 12
 COST = 1.0
 AFTER = ((), (), (), ("m0", "tm"), (), (), ())
 MIRROR_ROWS = (256,)

time: 97.4 us -> 109 us (1.12)
  the two profiles are of different devices: /device:TPU:1 before, /device:TPU:97 now
where the time goes in v4:
time: 109 us; the launch traced here: 108 us
  blocking collectives  31.1 us (29%)
  Pallas kernels  29.3 us (27%)
  starting transfers between devices  28.1 us (26%)
  waiting for transfers between devices  12 us (11%)
  local copies, waits for them, and re-layouts  6.88 us (6%)
    all_to_all x1, blocking collectives, gathered(): return lax.all_to_all(sums, 'tensor', 0, 0)  31.1 us
    pallas_call x6, Pallas kernels, call(): pl.pallas_call(body, name=name, out_shape=outs, in_specs=[SMEM if smem_fi...  25.8 us
    ppermute x1, waiting for transfers between devices, per_device(): lax.ppermute(jnp.broadcast_to(stored_squares, (8, TOK)), 'section', mirro...  12 us
    all_to_all x2, starting transfers between devices, gathered(): return lax.all_to_all(sums, 'tensor', 0, 0)  9.95 us
    unnamed x24, local copies, waits for them, and re-layouts  6.87 us
    ppermute x1, starting transfers between devices, per_device(): fetched.append(lax.ppermute(parked[at:at + rows_n], 'section', mirrored))  5.85 us
    ppermute x1, starting transfers between devices, per_device(): lax.ppermute(jnp.broadcast_to(stored_squares, (8, TOK)), 'section', mirro...  5.2 us
    ppermute x1, starting transfers between devices, per_device(): parked_out = [lax.ppermute(parking_out, 'section', parking)]  4.26 us
  transfers between devices with their start and end apart: 7, of which 1 were waited for; matrix products, arithmetic and copies ran while one was open for 0% of the time, Pallas kernels for 24%

profile of v4, /device:TPU:97, one launch (start us, length us, event | category | flops | bytes accessed | tf_op | source)
XLA Modules:
  0.0 108.3 jit_solution(1972322114408863972)
XLA Ops:
  0.6 0.0 copy-start
  0.6 0.0 copy-start.8
  0.7 0.0 copy-start.11
  0.7 0.0 copy-start.10
  0.7 0.0 copy-start.3
  0.7 2.6 %squares.1 = f32[8,8,256]{2,1,0:T(8,128)} custom-call(bf16[256,1536]{1,0:T(8,128)(2,1)} %bitcast.12, bf16[256,1536]{1,0:T(8,128)(2,1)} %bitcast.7, bf16[256,1536]{1,0:T(8,128)(2,1)} %bitcast.15), custom_call_target="tpu_custom_call" | custom-call | tf_op jit(solution)/shard_map/squares/pallas_call | solution.py:272
  3.3 5.1 %all-to-all-start = ((f32[8,8,256]{2,1,0:T(8,128)}), f32[8,8,256]{2,1,0:T(8,128)S(1)}, u32[]{:S(2)}, u32[]{:S(2)}) async-start(f32[8,8,256]{2,1,0:T(8,128)} %squares.1), calls=%async_computation | async-start | bytes 131072 | tf_op jit(solution)/shard_map/all_to_all | solution.py:360
  8.4 5.9 %collective-permute-start.1 = (bf16[256,1536]{1,0:T(8,128)(2,1)}, bf16[256,1536]{1,0:T(8,128)(2,1)S(1)}, u32[]{:S(2)}, u32[]{:S(2)}) collective-permute-start(bf16[256,1536]{1,0:T(8,128)(2,1)} %bitcast.16), channel_id=1, source_target_pairs={{0,248},{8,240},{16,232},{24,224},{32,216},{40,208},{48,200},{56,1... | collective-permute-start | bytes 2359304 | tf_op jit(solution)/shard_map/ppermute | solution.py:373
  14.3 0.0 all-to-all-done.refs_2_.refs_3_.refs_4_
  14.3 0.0 copy-done
  14.3 0.0 copy-done.8
  14.3 0.0 copy-done.11
  14.3 0.0 copy-done.10
  14.3 0.0 copy-done.3
  14.3 5.5 %backward_first.1 = (f32[256,1536]{1,0:T(8,128)S(1)}, f32[8,8,256]{2,1,0:T(8,128)}, f32[1,1536]{1,0:T(1,128)S(1)}, f32[1,1536]{1,0:T(1,128)S(1)}) custom-call(s32[65]{0:T(128)S(1)} %copy-done.8, bf16[256,1536]{1,0:T(8,128)(2,1)S(1)} %bitcast.8, bf16[256,1536]{1,0:T(8,128)(2,1)S(1)} %bitcast.10, f32[8,8,256]{2,1,0:T(8,128)S(1)} %all-to-all-done.refs_2_.refs_3_.refs_4_, ...), custom_call_target="tpu_custom_call" | custom-call | flops 6000000000 | bytes 3301636 | tf_op jit(solution)/shard_map/backward_first/pallas_call | solution.py:247
  19.8 0.0 copy-start.1
  19.8 1.2 %copy-done.1 = f32[256,1536]{1,0:T(8,128)} copy-done((f32[256,1536]{1,0:T(8,128)}, f32[256,1536]{1,0:T(8,128)S(1)}, u32[]{:S(2)}) %copy-start.1) | copy-done | bytes 1572888
  21.0 4.8 %all-to-all-start.1 = ((f32[8,8,256]{2,1,0:T(8,128)}), f32[8,8,256]{2,1,0:T(8,128)S(1)}, u32[]{:S(2)}, u32[]{:S(2)}) async-start(f32[8,8,256]{2,1,0:T(8,128)} %get-tuple-element.19), calls=%async_computation.1 | async-start | bytes 131072 | tf_op jit(solution)/shard_map/all_to_all | solution.py:360
  25.8 0.0 copy-start.5
  25.8 1.1 %copy-done.5 = bf16[1,256,1536]{2,1,0:T(8,128)(2,1)S(1)} copy-done((bf16[1,256,1536]{2,1,0:T(8,128)(2,1)S(1)}, bf16[1,256,1536]{2,1,0:T(8,128)(2,1)}, u32[]{:S(2)}) %copy-start.5) | copy-done | bytes 786456
  26.9 0.0 copy-start.9
  26.9 1.1 %copy-done.9 = bf16[256,1536]{1,0:T(8,128)(2,1)S(1)} copy-done((bf16[256,1536]{1,0:T(8,128)(2,1)S(1)}, bf16[256,1536]{1,0:T(8,128)(2,1)}, u32[]{:S(2)}) %copy-start.9) | copy-done | bytes 786456
  28.1 5.3 %forward_first.1 = (bf16[256,1536]{1,0:T(8,128)(2,1)}, bf16[256,1536]{1,0:T(8,128)(2,1)S(1)}) custom-call(s32[65]{0:T(128)S(1)} %copy-done.8, bf16[256,1536]{1,0:T(8,128)(2,1)S(1)} %bitcast.13, f32[8,8,256]{2,1,0:T(8,128)S(1)} %all-to-all-done.refs_2_.refs_3_.refs_4_, f32[1,1536]{1,0:T(1,128)S(1)} %copy-done.10, f32[1,1536]{1,0:T(1,128)S(1)} %copy-done.11, ...), custom_call_target="tpu_custom_call" | custom-call | flops 3000000000 | bytes 3223812 | tf_op jit(solution)/shard_map/forward_first/pallas_call | solution.py:247
  33.4 0.0 copy-start.6
  33.4 0.9 copy-done.6
  34.3 2.7 %collective-permute-start = (bf16[256,1536]{1,0:T(8,128)(2,1)}, bf16[256,1536]{1,0:T(8,128)(2,1)}, u32[]{:S(2)}, u32[]{:S(2)}) collective-permute-start(bf16[256,1536]{1,0:T(8,128)(2,1)} %get-tuple-element.17), channel_id=1, source_target_pairs={{0,8},{8,16},{16,24},{24,32},{32,40},{40,48},{48,56},{56,64},{64,7... | collective-permute-start | bytes 2359304 | tf_op jit(solution)/shard_map/ppermute | solution.py:401
  37.0 0.0 all-to-all-done.1.refs_5_
  37.0 0.0 copy-start.2
  37.0 1.4 %copy-done.2 = f32[256,1536]{1,0:T(8,128)S(1)} copy-done((f32[256,1536]{1,0:T(8,128)S(1)}, f32[256,1536]{1,0:T(8,128)}, u32[]{:S(2)}) %copy-start.2) | copy-done | bytes 1572888
  38.4 0.0 copy-start.4
  38.4 1.1 %copy-done.4 = bf16[256,1536]{1,0:T(8,128)(2,1)S(1)} copy-done((bf16[256,1536]{1,0:T(8,128)(2,1)S(1)}, bf16[256,1536]{1,0:T(8,128)(2,1)}, u32[]{:S(2)}) %copy-start.4) | copy-done | bytes 786456
  39.5 0.0 copy-start.7
  39.5 1.1 %finish_first.1 = bf16[256,1536]{1,0:T(8,128)(2,1)S(1)} custom-call(s32[65]{0:T(128)S(1)} %copy-done.8, bf16[256,1536]{1,0:T(8,128)(2,1)S(1)} %bitcast.9, bf16[256,1536]{1,0:T(8,128)(2,1)S(1)} %bitcast.11, f32[256,1536]{1,0:T(8,128)S(1)} %copy-done.2, f32[8,8,256]{2,1,0:T(8,128)S(1)} %all-to-all-done.refs_2_.refs_3_.refs_4_, ...), custom_call_target="tpu_custom_call" | custom-call | flops 1000000000 | bytes 4849924 | tf_op jit(solution)/shard_map/finish_first/pallas_call | solution.py:247
  40.7 0.1 collective-permute-start.2
  40.8 5.2 %collective-permute-start.3 = (f32[8,256]{1,0:T(8,128)S(1)}, f32[8,256]{1,0:T(8,128)S(1)}, u32[]{:S(2)}, u32[]{:S(2)}) collective-permute-start(f32[8,256]{1,0:T(8,128)S(1)} %broadcast_in_dim.15), channel_id=1, source_target_pairs={{0,248},{8,240},{16,232},{24,224},{32,216},{40,208},{48,200},{56,1... | collective-permute-start | bytes 24584 | tf_op jit(solution)/shard_map/ppermute | solution.py:382
  46.0 12.0 %collective-permute-done.3.refs_3_.refs_4_.refs_2_ = f32[8,256]{1,0:T(8,128)S(1)} collective-permute-done((f32[8,256]{1,0:T(8,128)S(1)}, f32[8,256]{1,0:T(8,128)S(1)}, u32[]{:S(2)}, u32[]{:S(2)}) %collective-permute-start.3) | collective-permute-done | bytes 8224 | tf_op jit(solution)/shard_map/ppermute | solution.py:382
  58.0 0.0 collective-permute-done.1.refs_1_
  58.0 0.0 copy-done.7
  58.0 4.3 %collective-permute-start.4 = (bf16[256,1536]{1,0:T(8,128)(2,1)S(1)}, bf16[256,1536]{1,0:T(8,128)(2,1)S(1)}, u32[]{:S(2)}, u32[]{:S(2)}) collective-permute-start(bf16[256,1536]{1,0:T(8,128)(2,1)S(1)} %hold.1), channel_id=1, source_target_pairs={{0,240},{8,232},{16,224},{24,216},{32,208},{40,200},{48,192},{56,1... | collective-permute-start | bytes 2359304 | tf_op jit(solution)/shard_map/ppermute | solution.py:403
  62.3 0.0 collective-permute-done.refs_8_.refs_1_
  62.3 0.0 collective-permute-done.2.refs_2_
  62.3 6.0 %backward_second.1 = (f32[256,1536]{1,0:T(8,128)S(1)}, f32[8,8,256]{2,1,0:T(8,128)S(1)}, f32[1,1536]{1,0:T(1,128)}, f32[1,1536]{1,0:T(1,128)}) custom-call(s32[65]{0:T(128)S(1)} %copy-done.8, bf16[256,1536]{1,0:T(8,128)(2,1)S(1)} %collective-permute-done.1.refs_1_, bf16[256,1536]{1,0:T(8,128)(2,1)S(1)} %collective-permute-done.2.refs_2_, ...), custom_call_target="tpu_custom_call" | custom-call | flops 6000000000 | bytes 4043012 | tf_op jit(solution)/shard_map/backward_second/pallas_call | solution.py:247
  68.3 31.1 %all_to_all.15.refs_2_.refs_5_ = f32[8,8,256]{2,1,0:T(8,128)S(1)} all-to-all(f32[8,8,256]{2,1,0:T(8,128)S(1)} %get-tuple-element.22), channel_id=1, replica_groups=mesh['section'=32,'tensor'=8] {'tensor'}, dimensions={0} | all-to-all | bytes 131072 | tf_op jit(solution)/shard_map/all_to_all | solution.py:360
  99.4 1.9 %finish_second.1 = bf16[256,1536]{1,0:T(8,128)(2,1)} custom-call(s32[65]{0:T(128)S(1)} %copy-done.8, bf16[256,1536]{1,0:T(8,128)(2,1)S(1)} %collective-permute-done.1.refs_1_, bf16[256,1536]{1,0:T(8,128)(2,1)S(1)} %collective-permute-done.2.refs_2_, f32[256,1536]{1,0:T(8,128)S(1)} %get-tuple-element.24.refs_3_, ...), custom_call_target="tpu_custom_call" | custom-call | flops 1000000000 | bytes 4006148 | tf_op jit(solution)/shard_map/finish_second/pallas_call | solution.py:247
  101.3 5.9 %forward_second.1 = (bf16[256,1536]{1,0:T(8,128)(2,1)}, f32[8,128]{1,0:T(8,128)S(1)}) custom-call(s32[65]{0:T(128)S(1)} %copy-done.8, bf16[256,1536]{1,0:T(8,128)(2,1)} %collective-permute-done.refs_8_.refs_1_, f32[8,8,256]{2,1,0:T(8,128)S(1)} %all_to_all.15.refs_2_.refs_5_, f32[1,1536]{1,0:T(1,128)S(1)} %copy-done.10, f32[1,1536]{1,0:T(1,128)S(1)} %copy-done.11), custom_call_target="tpu_custom_call" | custom-call | flops 3000000000 | bytes 1655044 | tf_op jit(solution)/shard_map/forward_second/pallas_call | solution.py:247
  107.3 0.0 collective-permute-done.4.refs_0_
  107.3 0.9 settle.1
  (3 shorter events, 0.0 us)
Async XLA Ops:
  0.6 13.7 %copy-start = (bf16[1,256,1536]{2,1,0:T(8,128)(2,1)S(1)}, bf16[1,256,1536]{2,1,0:T(8,128)(2,1)}, u32[]{:S(2)}) copy-start(bf16[1,256,1536]{2,1,0:T(8,128)(2,1)} %param.11) | copy-start | bytes 2359300
  0.6 13.6 %copy-start.8 = (s32[65]{0:T(128)S(1)}, s32[65]{0:T(128)}, u32[]{:S(2)}) copy-start(s32[65]{0:T(128)} %refs_0_.11) | copy-start | bytes 784
  0.7 13.6 %copy-start.11 = (f32[1,1536]{1,0:T(1,128)S(1)}, f32[1,1536]{1,0:T(1,128)}, u32[]{:S(2)}) copy-start(f32[1,1536]{1,0:T(1,128)} %refs_4_.7) | copy-start | bytes 18436
  0.7 13.6 %copy-start.10 = (f32[1,1536]{1,0:T(1,128)S(1)}, f32[1,1536]{1,0:T(1,128)}, u32[]{:S(2)}) copy-start(f32[1,1536]{1,0:T(1,128)} %refs_3_.3) | copy-start | bytes 18436
  0.7 13.6 %copy-start.3 = (bf16[1,256,1536]{2,1,0:T(8,128)(2,1)S(1)}, bf16[1,256,1536]{2,1,0:T(8,128)(2,1)}, u32[]{:S(2)}) copy-start(bf16[1,256,1536]{2,1,0:T(8,128)(2,1)} %param.10) | copy-start | bytes 2359300
  3.3 11.0 %all-to-all-start = ((f32[8,8,256]{2,1,0:T(8,128)}), f32[8,8,256]{2,1,0:T(8,128)S(1)}, u32[]{:S(2)}, u32[]{:S(2)}) async-start(f32[8,8,256]{2,1,0:T(8,128)} %squares.1), calls=%async_computation | async-start | bytes 131072 | tf_op jit(solution)/shard_map/all_to_all | solution.py:360
  8.4 49.6 %collective-permute-start.1 = (bf16[256,1536]{1,0:T(8,128)(2,1)}, bf16[256,1536]{1,0:T(8,128)(2,1)S(1)}, u32[]{:S(2)}, u32[]{:S(2)}) collective-permute-start(bf16[256,1536]{1,0:T(8,128)(2,1)} %bitcast.16), channel_id=1, source_target_pairs={{0,248},{8,240},{16,232},{24,224},{32,216},{40,208},{48,200},{56,1... | collective-permute-start | bytes 2359304 | tf_op jit(solution)/shard_map/ppermute | solution.py:373
  19.8 1.2 %copy-start.1 = (f32[256,1536]{1,0:T(8,128)}, f32[256,1536]{1,0:T(8,128)S(1)}, u32[]{:S(2)}) copy-start(f32[256,1536]{1,0:T(8,128)S(1)} %get-tuple-element.18.refs_3_) | copy-start | bytes 4718596
  21.0 16.0 %all-to-all-start.1 = ((f32[8,8,256]{2,1,0:T(8,128)}), f32[8,8,256]{2,1,0:T(8,128)S(1)}, u32[]{:S(2)}, u32[]{:S(2)}) async-start(f32[8,8,256]{2,1,0:T(8,128)} %get-tuple-element.19), calls=%async_computation.1 | async-start | bytes 131072 | tf_op jit(solution)/shard_map/all_to_all | solution.py:360
  25.8 1.1 %copy-start.5 = (bf16[1,256,1536]{2,1,0:T(8,128)(2,1)S(1)}, bf16[1,256,1536]{2,1,0:T(8,128)(2,1)}, u32[]{:S(2)}) copy-start(bf16[1,256,1536]{2,1,0:T(8,128)(2,1)} %param.9) | copy-start | bytes 2359300
  26.9 1.1 %copy-start.9 = (bf16[256,1536]{1,0:T(8,128)(2,1)S(1)}, bf16[256,1536]{1,0:T(8,128)(2,1)}, u32[]{:S(2)}) copy-start(bf16[256,1536]{1,0:T(8,128)(2,1)} %refs_5_.3) | copy-start | bytes 2359300
  33.4 0.9 copy-start.6
  34.3 28.0 %collective-permute-start = (bf16[256,1536]{1,0:T(8,128)(2,1)}, bf16[256,1536]{1,0:T(8,128)(2,1)}, u32[]{:S(2)}, u32[]{:S(2)}) collective-permute-start(bf16[256,1536]{1,0:T(8,128)(2,1)} %get-tuple-element.17), channel_id=1, source_target_pairs={{0,8},{8,16},{16,24},{24,32},{32,40},{40,48},{48,56},{56,64},{64,7... | collective-permute-start | bytes 2359304 | tf_op jit(solution)/shard_map/ppermute | solution.py:401
  37.0 1.4 %copy-start.2 = (f32[256,1536]{1,0:T(8,128)S(1)}, f32[256,1536]{1,0:T(8,128)}, u32[]{:S(2)}) copy-start(f32[256,1536]{1,0:T(8,128)} %copy-done.1) | copy-start | bytes 4718596
  38.4 1.1 %copy-start.4 = (bf16[256,1536]{1,0:T(8,128)(2,1)S(1)}, bf16[256,1536]{1,0:T(8,128)(2,1)}, u32[]{:S(2)}) copy-start(bf16[256,1536]{1,0:T(8,128)(2,1)} %refs_6_.1) | copy-start | bytes 2359300
  39.5 18.5 %copy-start.7 = (bf16[256,1536]{1,0:T(8,128)(2,1)S(1)}, bf16[256,1536]{1,0:T(8,128)(2,1)}, u32[]{:S(2)}) copy-start(bf16[256,1536]{1,0:T(8,128)(2,1)} %copy-done.6) | copy-start | bytes 2359300
  40.7 21.6 %collective-permute-start.2 = (bf16[256,1536]{1,0:T(8,128)(2,1)S(1)}, bf16[256,1536]{1,0:T(8,128)(2,1)S(1)}, u32[]{:S(2)}, u32[]{:S(2)}) collective-permute-start(bf16[256,1536]{1,0:T(8,128)(2,1)S(1)} %finish_first.1), channel_id=1, source_target_pairs={{8,0},{16,8},{24,16},{32,24},{40,32},{48,40},{56,48},{64,56},{72,6... | collective-permute-start | bytes 2359304 | tf_op jit(solution)/shard_map/ppermute | solution.py:393
  40.8 17.2 %collective-permute-start.3 = (f32[8,256]{1,0:T(8,128)S(1)}, f32[8,256]{1,0:T(8,128)S(1)}, u32[]{:S(2)}, u32[]{:S(2)}) collective-permute-start(f32[8,256]{1,0:T(8,128)S(1)} %broadcast_in_dim.15), channel_id=1, source_target_pairs={{0,248},{8,240},{16,232},{24,224},{32,216},{40,208},{48,200},{56,1... | collective-permute-start | bytes 24584 | tf_op jit(solution)/shard_map/ppermute | solution.py:382
  58.0 49.3 %collective-permute-start.4 = (bf16[256,1536]{1,0:T(8,128)(2,1)S(1)}, bf16[256,1536]{1,0:T(8,128)(2,1)S(1)}, u32[]{:S(2)}, u32[]{:S(2)}) collective-permute-start(bf16[256,1536]{1,0:T(8,128)(2,1)S(1)} %hold.1), channel_id=1, source_target_pairs={{0,240},{8,232},{16,224},{24,216},{32,208},{40,200},{48,192},{56,1... | collective-permute-start | bytes 2359304 | tf_op jit(solution)/shard_map/ppermute | solution.py:403

commit v5 on v3

--- a/solution.py
+++ b/solution.py
@@ -19,7 +19,7 @@
 WHOLE_VMEM = 62 * 1024 * 1024
 UNROLL = 6
 COST = 1.0
-AFTER = ((), (), (), ("m0", "tm"), (), (), ())
+AFTER = ((), (), (), ("m0", "tm", "x"), (), (), ())
 MIRROR_ROWS = (256,)
 HOLD = True
 
@@ -395,11 +395,11 @@
     first_out, parking_out = forward_first(
         lambda s: 2 * count - 1 - s, lengths, x, sums, gain, qgain, fresh, after(2)
     )
-    if HOLD:
-        parking_out = hold(parking_out, after(3))
     made["y1"] = first_out
     x_two = lax.ppermute(first_out, "section", onward)
     made["x"] = x_two
+    if HOLD:
+        parking_out = hold(parking_out, after(3))
     parked_out = [lax.ppermute(parking_out, "section", parking)]
     d_unit, project, gain_two, qgain_two = backward_call(
         lambda s: s + 1, False, lengths, fetched, d_two, stored_squares, gain, qgain,

time: 97.4 us -> 97.4 us (level)
  no operation moved by 1% of the time
where the time goes in v5:
time: 97.4 us; the launch traced here: 96.8 us
  starting transfers between devices  36.8 us (38%)
  Pallas kernels  30.2 us (31%)
  waiting for transfers between devices  11.2 us (11%)
  blocking collectives  11 us (11%)
  local copies, waits for them, and re-layouts  6.88 us (7%)
    pallas_call x6, Pallas kernels, call(): pl.pallas_call(body, name=name, out_shape=outs, in_specs=[SMEM if smem_fi...  26.8 us
    all_to_all x1, blocking collectives, gathered(): return lax.all_to_all(sums, 'tensor', 0, 0)  11 us
    all_to_all x2, starting transfers between devices, gathered(): return lax.all_to_all(sums, 'tensor', 0, 0)  10.8 us
    ppermute x1, starting transfers between devices, per_device(): parked_out = [lax.ppermute(parking_out, 'section', parking)]  9.4 us
    ppermute x1, starting transfers between devices, per_device(): fetched.append(lax.ppermute(parked[at:at + rows_n], 'section', mirrored))  8.58 us
    ppermute x1, waiting for transfers between devices, per_device(): parked_out = [lax.ppermute(parking_out, 'section', parking)]  8.16 us
    unnamed x24, local copies, waits for them, and re-layouts  6.87 us
    ppermute x1, starting transfers between devices, per_device(): lax.ppermute(jnp.broadcast_to(stored_squares, (8, TOK)), 'section', mirro...  6.85 us
  transfers between devices with their start and end apart: 7, of which 2 were waited for; matrix products, arithmetic and copies ran while one was open for 0% of the time, Pallas kernels for 28%

profile of v5, /device:TPU:1, one launch (start us, length us, event | category | flops | bytes accessed | tf_op | source)
XLA Modules:
  0.0 96.8 jit_solution(2722465688137791100)
XLA Ops:
  0.6 0.0 copy-start
  0.6 0.0 copy-start.8
  0.7 0.0 copy-start.11
  0.7 0.0 copy-start.10
  0.7 0.0 copy-start.3
  0.7 2.6 %squares.1 = f32[8,8,256]{2,1,0:T(8,128)} custom-call(bf16[256,1536]{1,0:T(8,128)(2,1)} %bitcast.12, bf16[256,1536]{1,0:T(8,128)(2,1)} %bitcast.7, bf16[256,1536]{1,0:T(8,128)(2,1)} %bitcast.15), custom_call_target="tpu_custom_call" | custom-call | tf_op jit(solution)/shard_map/squares/pallas_call | solution.py:272
  3.3 6.0 %all-to-all-start = ((f32[8,8,256]{2,1,0:T(8,128)}), f32[8,8,256]{2,1,0:T(8,128)S(1)}, u32[]{:S(2)}, u32[]{:S(2)}) async-start(f32[8,8,256]{2,1,0:T(8,128)} %squares.1), calls=%async_computation | async-start | bytes 131072 | tf_op jit(solution)/shard_map/all_to_all | solution.py:360
  9.3 8.6 %collective-permute-start.1 = (bf16[256,1536]{1,0:T(8,128)(2,1)}, bf16[256,1536]{1,0:T(8,128)(2,1)S(1)}, u32[]{:S(2)}, u32[]{:S(2)}) collective-permute-start(bf16[256,1536]{1,0:T(8,128)(2,1)} %bitcast.16), channel_id=1, source_target_pairs={{0,248},{8,240},{16,232},{24,224},{32,216},{40,208},{48,200},{56,1... | collective-permute-start | bytes 2359304 | tf_op jit(solution)/shard_map/ppermute | solution.py:373
  17.8 0.0 all-to-all-done.refs_2_.refs_3_.refs_4_
  17.8 0.0 copy-done
  17.8 0.0 copy-done.8
  17.9 0.0 copy-done.11
  17.9 0.0 copy-done.10
  17.9 0.0 copy-done.3
  17.9 5.8 %backward_first.1 = (f32[256,1536]{1,0:T(8,128)S(1)}, f32[8,8,256]{2,1,0:T(8,128)}, f32[1,1536]{1,0:T(1,128)S(1)}, f32[1,1536]{1,0:T(1,128)S(1)}) custom-call(s32[65]{0:T(128)S(1)} %copy-done.8, bf16[256,1536]{1,0:T(8,128)(2,1)S(1)} %bitcast.8, bf16[256,1536]{1,0:T(8,128)(2,1)S(1)} %bitcast.10, f32[8,8,256]{2,1,0:T(8,128)S(1)} %all-to-all-done.refs_2_.refs_3_.refs_4_, ...), custom_call_target="tpu_custom_call" | custom-call | flops 6000000000 | bytes 3301636 | tf_op jit(solution)/shard_map/backward_first/pallas_call | solution.py:247
  23.7 0.0 copy-start.1
  23.7 1.2 %copy-done.1 = f32[256,1536]{1,0:T(8,128)} copy-done((f32[256,1536]{1,0:T(8,128)}, f32[256,1536]{1,0:T(8,128)S(1)}, u32[]{:S(2)}) %copy-start.1) | copy-done | bytes 1572888
  24.8 4.8 %all-to-all-start.1 = ((f32[8,8,256]{2,1,0:T(8,128)}), f32[8,8,256]{2,1,0:T(8,128)S(1)}, u32[]{:S(2)}, u32[]{:S(2)}) async-start(f32[8,8,256]{2,1,0:T(8,128)} %get-tuple-element.19), calls=%async_computation.1 | async-start | bytes 131072 | tf_op jit(solution)/shard_map/all_to_all | solution.py:360
  29.6 0.0 copy-start.5
  29.6 1.1 %copy-done.5 = bf16[1,256,1536]{2,1,0:T(8,128)(2,1)S(1)} copy-done((bf16[1,256,1536]{2,1,0:T(8,128)(2,1)S(1)}, bf16[1,256,1536]{2,1,0:T(8,128)(2,1)}, u32[]{:S(2)}) %copy-start.5) | copy-done | bytes 786456
  30.8 0.0 copy-start.9
  30.8 1.1 %copy-done.9 = bf16[256,1536]{1,0:T(8,128)(2,1)S(1)} copy-done((bf16[256,1536]{1,0:T(8,128)(2,1)S(1)}, bf16[256,1536]{1,0:T(8,128)(2,1)}, u32[]{:S(2)}) %copy-start.9) | copy-done | bytes 786456
  31.9 5.5 %forward_first.1 = (bf16[256,1536]{1,0:T(8,128)(2,1)}, bf16[256,1536]{1,0:T(8,128)(2,1)S(1)}) custom-call(s32[65]{0:T(128)S(1)} %copy-done.8, bf16[256,1536]{1,0:T(8,128)(2,1)S(1)} %bitcast.13, f32[8,8,256]{2,1,0:T(8,128)S(1)} %all-to-all-done.refs_2_.refs_3_.refs_4_, f32[1,1536]{1,0:T(1,128)S(1)} %copy-done.10, f32[1,1536]{1,0:T(1,128)S(1)} %copy-done.11, ...), custom_call_target="tpu_custom_call" | custom-call | flops 3000000000 | bytes 3223812 | tf_op jit(solution)/shard_map/forward_first/pallas_call | solution.py:247
  37.5 0.0 copy-start.6
  37.5 0.9 copy-done.6
  38.3 1.1 %collective-permute-start = (bf16[256,1536]{1,0:T(8,128)(2,1)}, bf16[256,1536]{1,0:T(8,128)(2,1)}, u32[]{:S(2)}, u32[]{:S(2)}) collective-permute-start(bf16[256,1536]{1,0:T(8,128)(2,1)} %get-tuple-element.17), channel_id=1, source_target_pairs={{0,8},{8,16},{16,24},{24,32},{32,40},{40,48},{48,56},{56,64},{64,7... | collective-permute-start | bytes 2359304 | tf_op jit(solution)/shard_map/ppermute | solution.py:399
  39.4 0.0 all-to-all-done.1.refs_5_
  39.4 0.0 copy-start.2
  39.4 1.4 %copy-done.2 = f32[256,1536]{1,0:T(8,128)S(1)} copy-done((f32[256,1536]{1,0:T(8,128)S(1)}, f32[256,1536]{1,0:T(8,128)}, u32[]{:S(2)}) %copy-start.2) | copy-done | bytes 1572888
  40.8 0.0 copy-start.4
  40.8 1.1 %copy-done.4 = bf16[256,1536]{1,0:T(8,128)(2,1)S(1)} copy-done((bf16[256,1536]{1,0:T(8,128)(2,1)S(1)}, bf16[256,1536]{1,0:T(8,128)(2,1)}, u32[]{:S(2)}) %copy-start.4) | copy-done | bytes 786456
  42.0 0.0 copy-start.7
  42.0 1.1 %finish_first.1 = bf16[256,1536]{1,0:T(8,128)(2,1)S(1)} custom-call(s32[65]{0:T(128)S(1)} %copy-done.8, bf16[256,1536]{1,0:T(8,128)(2,1)S(1)} %bitcast.9, bf16[256,1536]{1,0:T(8,128)(2,1)S(1)} %bitcast.11, f32[256,1536]{1,0:T(8,128)S(1)} %copy-done.2, f32[8,8,256]{2,1,0:T(8,128)S(1)} %all-to-all-done.refs_2_.refs_3_.refs_4_, ...), custom_call_target="tpu_custom_call" | custom-call | flops 1000000000 | bytes 4849924 | tf_op jit(solution)/shard_map/finish_first/pallas_call | solution.py:247
  43.1 0.1 collective-permute-start.2
  43.2 6.9 %collective-permute-start.3 = (f32[8,256]{1,0:T(8,128)S(1)}, f32[8,256]{1,0:T(8,128)S(1)}, u32[]{:S(2)}, u32[]{:S(2)}) collective-permute-start(f32[8,256]{1,0:T(8,128)S(1)} %broadcast_in_dim.15), channel_id=1, source_target_pairs={{0,248},{8,240},{16,232},{24,224},{32,216},{40,208},{48,200},{56,1... | collective-permute-start | bytes 24584 | tf_op jit(solution)/shard_map/ppermute | solution.py:382
  50.1 3.0 %collective-permute-done.3.refs_3_.refs_4_.refs_2_ = f32[8,256]{1,0:T(8,128)S(1)} collective-permute-done((f32[8,256]{1,0:T(8,128)S(1)}, f32[8,256]{1,0:T(8,128)S(1)}, u32[]{:S(2)}, u32[]{:S(2)}) %collective-permute-start.3) | collective-permute-done | bytes 8224 | tf_op jit(solution)/shard_map/ppermute | solution.py:382
  53.1 0.0 collective-permute-done.1.refs_1_
  53.1 0.0 collective-permute-done.refs_8_.refs_1_.refs_3_
  53.1 0.0 copy-done.7
  53.1 9.4 %collective-permute-start.4 = (bf16[256,1536]{1,0:T(8,128)(2,1)S(1)}, bf16[256,1536]{1,0:T(8,128)(2,1)S(1)}, u32[]{:S(2)}, u32[]{:S(2)}) collective-permute-start(bf16[256,1536]{1,0:T(8,128)(2,1)S(1)} %hold.1), channel_id=1, source_target_pairs={{0,240},{8,232},{16,224},{24,216},{32,208},{40,200},{48,192},{56,1... | collective-permute-start | bytes 2359304 | tf_op jit(solution)/shard_map/ppermute | solution.py:403
  62.5 0.0 collective-permute-done.2.refs_2_
  62.5 6.2 %backward_second.1 = (f32[256,1536]{1,0:T(8,128)S(1)}, f32[8,8,256]{2,1,0:T(8,128)S(1)}, f32[1,1536]{1,0:T(1,128)}, f32[1,1536]{1,0:T(1,128)}) custom-call(s32[65]{0:T(128)S(1)} %copy-done.8, bf16[256,1536]{1,0:T(8,128)(2,1)S(1)} %collective-permute-done.1.refs_1_, bf16[256,1536]{1,0:T(8,128)(2,1)S(1)} %collective-permute-done.2.refs_2_, ...), custom_call_target="tpu_custom_call" | custom-call | flops 6000000000 | bytes 4043012 | tf_op jit(solution)/shard_map/backward_second/pallas_call | solution.py:247
  68.7 11.0 %all_to_all.15.refs_2_.refs_5_ = f32[8,8,256]{2,1,0:T(8,128)S(1)} all-to-all(f32[8,8,256]{2,1,0:T(8,128)S(1)} %get-tuple-element.22), channel_id=1, replica_groups=mesh['section'=32,'tensor'=8] {'tensor'}, dimensions={0} | all-to-all | bytes 131072 | tf_op jit(solution)/shard_map/all_to_all | solution.py:360
  79.7 1.9 %finish_second.1 = bf16[256,1536]{1,0:T(8,128)(2,1)} custom-call(s32[65]{0:T(128)S(1)} %copy-done.8, bf16[256,1536]{1,0:T(8,128)(2,1)S(1)} %collective-permute-done.1.refs_1_, bf16[256,1536]{1,0:T(8,128)(2,1)S(1)} %collective-permute-done.2.refs_2_, f32[256,1536]{1,0:T(8,128)S(1)} %get-tuple-element.24.refs_3_, ...), custom_call_target="tpu_custom_call" | custom-call | flops 1000000000 | bytes 4006148 | tf_op jit(solution)/shard_map/finish_second/pallas_call | solution.py:247
  81.6 6.1 %forward_second.1 = (bf16[256,1536]{1,0:T(8,128)(2,1)}, f32[8,128]{1,0:T(8,128)S(1)}) custom-call(s32[65]{0:T(128)S(1)} %copy-done.8, bf16[256,1536]{1,0:T(8,128)(2,1)} %collective-permute-done.refs_8_.refs_1_.refs_3_, f32[8,8,256]{2,1,0:T(8,128)S(1)} %all_to_all.15.refs_2_.refs_5_, f32[1,1536]{1,0:T(1,128)S(1)} %copy-done.10, f32[1,1536]{1,0:T(1,128)S(1)} %copy-done.11), custom_call_target="tpu_custom_call" | custom-call | flops 3000000000 | bytes 1655044 | tf_op jit(solution)/shard_map/forward_second/pallas_call | solution.py:247
  87.8 8.2 %collective-permute-done.4.refs_0_ = bf16[256,1536]{1,0:T(8,128)(2,1)S(1)} collective-permute-done((bf16[256,1536]{1,0:T(8,128)(2,1)S(1)}, bf16[256,1536]{1,0:T(8,128)(2,1)S(1)}, u32[]{:S(2)}, u32[]{:S(2)}) %collective-permute-start.4) | collective-permute-done | bytes 786464 | tf_op jit(solution)/shard_map/ppermute | solution.py:403
  96.0 0.9 settle.1
  (3 shorter events, 0.0 us)
Async XLA Ops:
  0.6 17.2 %copy-start = (bf16[1,256,1536]{2,1,0:T(8,128)(2,1)S(1)}, bf16[1,256,1536]{2,1,0:T(8,128)(2,1)}, u32[]{:S(2)}) copy-start(bf16[1,256,1536]{2,1,0:T(8,128)(2,1)} %param.11) | copy-start | bytes 2359300
  0.6 17.2 %copy-start.8 = (s32[65]{0:T(128)S(1)}, s32[65]{0:T(128)}, u32[]{:S(2)}) copy-start(s32[65]{0:T(128)} %refs_0_.11) | copy-start | bytes 784
  0.7 17.2 %copy-start.11 = (f32[1,1536]{1,0:T(1,128)S(1)}, f32[1,1536]{1,0:T(1,128)}, u32[]{:S(2)}) copy-start(f32[1,1536]{1,0:T(1,128)} %refs_4_.7) | copy-start | bytes 18436
  0.7 17.2 %copy-start.10 = (f32[1,1536]{1,0:T(1,128)S(1)}, f32[1,1536]{1,0:T(1,128)}, u32[]{:S(2)}) copy-start(f32[1,1536]{1,0:T(1,128)} %refs_3_.3) | copy-start | bytes 18436
  0.7 17.2 %copy-start.3 = (bf16[1,256,1536]{2,1,0:T(8,128)(2,1)S(1)}, bf16[1,256,1536]{2,1,0:T(8,128)(2,1)}, u32[]{:S(2)}) copy-start(bf16[1,256,1536]{2,1,0:T(8,128)(2,1)} %param.10) | copy-start | bytes 2359300
  3.3 14.5 %all-to-all-start = ((f32[8,8,256]{2,1,0:T(8,128)}), f32[8,8,256]{2,1,0:T(8,128)S(1)}, u32[]{:S(2)}, u32[]{:S(2)}) async-start(f32[8,8,256]{2,1,0:T(8,128)} %squares.1), calls=%async_computation | async-start | bytes 131072 | tf_op jit(solution)/shard_map/all_to_all | solution.py:360
  9.3 43.8 %collective-permute-start.1 = (bf16[256,1536]{1,0:T(8,128)(2,1)}, bf16[256,1536]{1,0:T(8,128)(2,1)S(1)}, u32[]{:S(2)}, u32[]{:S(2)}) collective-permute-start(bf16[256,1536]{1,0:T(8,128)(2,1)} %bitcast.16), channel_id=1, source_target_pairs={{0,248},{8,240},{16,232},{24,224},{32,216},{40,208},{48,200},{56,1... | collective-permute-start | bytes 2359304 | tf_op jit(solution)/shard_map/ppermute | solution.py:373
  23.7 1.2 %copy-start.1 = (f32[256,1536]{1,0:T(8,128)}, f32[256,1536]{1,0:T(8,128)S(1)}, u32[]{:S(2)}) copy-start(f32[256,1536]{1,0:T(8,128)S(1)} %get-tuple-element.18.refs_3_) | copy-start | bytes 4718596
  24.8 14.6 %all-to-all-start.1 = ((f32[8,8,256]{2,1,0:T(8,128)}), f32[8,8,256]{2,1,0:T(8,128)S(1)}, u32[]{:S(2)}, u32[]{:S(2)}) async-start(f32[8,8,256]{2,1,0:T(8,128)} %get-tuple-element.19), calls=%async_computation.1 | async-start | bytes 131072 | tf_op jit(solution)/shard_map/all_to_all | solution.py:360
  29.6 1.1 %copy-start.5 = (bf16[1,256,1536]{2,1,0:T(8,128)(2,1)S(1)}, bf16[1,256,1536]{2,1,0:T(8,128)(2,1)}, u32[]{:S(2)}) copy-start(bf16[1,256,1536]{2,1,0:T(8,128)(2,1)} %param.9) | copy-start | bytes 2359300
  30.8 1.1 %copy-start.9 = (bf16[256,1536]{1,0:T(8,128)(2,1)S(1)}, bf16[256,1536]{1,0:T(8,128)(2,1)}, u32[]{:S(2)}) copy-start(bf16[256,1536]{1,0:T(8,128)(2,1)} %refs_5_.3) | copy-start | bytes 2359300
  37.5 0.9 copy-start.6
  38.3 14.8 %collective-permute-start = (bf16[256,1536]{1,0:T(8,128)(2,1)}, bf16[256,1536]{1,0:T(8,128)(2,1)}, u32[]{:S(2)}, u32[]{:S(2)}) collective-permute-start(bf16[256,1536]{1,0:T(8,128)(2,1)} %get-tuple-element.17), channel_id=1, source_target_pairs={{0,8},{8,16},{16,24},{24,32},{32,40},{40,48},{48,56},{56,64},{64,7... | collective-permute-start | bytes 2359304 | tf_op jit(solution)/shard_map/ppermute | solution.py:399
  39.4 1.4 %copy-start.2 = (f32[256,1536]{1,0:T(8,128)S(1)}, f32[256,1536]{1,0:T(8,128)}, u32[]{:S(2)}) copy-start(f32[256,1536]{1,0:T(8,128)} %copy-done.1) | copy-start | bytes 4718596
  40.8 1.1 %copy-start.4 = (bf16[256,1536]{1,0:T(8,128)(2,1)S(1)}, bf16[256,1536]{1,0:T(8,128)(2,1)}, u32[]{:S(2)}) copy-start(bf16[256,1536]{1,0:T(8,128)(2,1)} %refs_6_.1) | copy-start | bytes 2359300
  42.0 11.1 %copy-start.7 = (bf16[256,1536]{1,0:T(8,128)(2,1)S(1)}, bf16[256,1536]{1,0:T(8,128)(2,1)}, u32[]{:S(2)}) copy-start(bf16[256,1536]{1,0:T(8,128)(2,1)} %copy-done.6) | copy-start | bytes 2359300
  43.1 19.4 %collective-permute-start.2 = (bf16[256,1536]{1,0:T(8,128)(2,1)S(1)}, bf16[256,1536]{1,0:T(8,128)(2,1)S(1)}, u32[]{:S(2)}, u32[]{:S(2)}) collective-permute-start(bf16[256,1536]{1,0:T(8,128)(2,1)S(1)} %finish_first.1), channel_id=1, source_target_pairs={{8,0},{16,8},{24,16},{32,24},{40,32},{48,40},{56,48},{64,56},{72,6... | collective-permute-start | bytes 2359304 | tf_op jit(solution)/shard_map/ppermute | solution.py:393
  43.2 9.9 %collective-permute-start.3 = (f32[8,256]{1,0:T(8,128)S(1)}, f32[8,256]{1,0:T(8,128)S(1)}, u32[]{:S(2)}, u32[]{:S(2)}) collective-permute-start(f32[8,256]{1,0:T(8,128)S(1)} %broadcast_in_dim.15), channel_id=1, source_target_pairs={{0,248},{8,240},{16,232},{24,224},{32,216},{40,208},{48,200},{56,1... | collective-permute-start | bytes 24584 | tf_op jit(solution)/shard_map/ppermute | solution.py:382
  53.1 42.8 %collective-permute-start.4 = (bf16[256,1536]{1,0:T(8,128)(2,1)S(1)}, bf16[256,1536]{1,0:T(8,128)(2,1)S(1)}, u32[]{:S(2)}, u32[]{:S(2)}) collective-permute-start(bf16[256,1536]{1,0:T(8,128)(2,1)S(1)} %hold.1), channel_id=1, source_target_pairs={{0,240},{8,232},{16,224},{24,216},{32,208},{40,200},{48,192},{56,1... | collective-permute-start | bytes 2359304 | tf_op jit(solution)/shard_map/ppermute | solution.py:403
